TPU v7x, 32 devices: a whole 2x2x4 slice. The times are simulated.
32 devices in a mesh: row: 8 (over z, y), col: 4 (over x, core).
Axes of the slice: x: 2, y: 2, z: 4, core: 2. Of those that a mesh axis runs over, the one named last changes fastest.
Arguments:
- tokens: bfloat16 [1024, 8192], P('row', 'col'), may hold values from -6 to 6
- w_gate: bfloat16 [8192, 14336], P('col', 'row'), may hold values from -0.0625 to 0.0625
- w_up: bfloat16 [8192, 14336], P('col', 'row'), may hold values from -0.0625 to 0.0625
- w_down: bfloat16 [14336, 8192], P('row', 'col'), may hold values from -0.046875 to 0.046875
- cotangent: bfloat16 [1024, 8192], P('row', 'col'), may hold values from -0.5 to 0.5
Outputs:
- mixed: bfloat16 [1024, 8192], P('row', 'col')
- grad_gate: bfloat16 [8192, 14336], P('col', 'row')
- grad_up: bfloat16 [8192, 14336], P('col', 'row')
- grad_down: bfloat16 [14336, 8192], P('row', 'col')
All inputs are finite; a program needn't handle non-finite values.
Results may differ from a plain program's by a relative error of at most 0.04.
Values may be sent and summed in bfloat16 or wider, within the bound.
A program may use at most 128 MiB of HBM per device.

v0:
```python
import jax
import jax.numpy as jnp
from jax import lax
from jax.sharding import PartitionSpec as P


def over_tokens(left, right):
    return lax.dot_general(
        left, right, (((0,), (0,)), ((), ())), preferred_element_type=jnp.float32
    )


def gate_step(gate_sum):
    sigmoid_gate = jax.nn.sigmoid(gate_sum)
    return (sigmoid_gate, gate_sum * sigmoid_gate)


def backward_step(hidden_grad, gate_sum, up_sum):
    sigmoid_gate, silu_gate = gate_step(gate_sum)
    pre_gate = (
        hidden_grad * up_sum * sigmoid_gate * (1.0 + gate_sum * (1.0 - sigmoid_gate))
    ).astype(jnp.bfloat16)
    pre_up = (hidden_grad * silu_gate).astype(jnp.bfloat16)
    return (pre_gate, pre_up)


def local(tokens, w_gate, w_up, w_down, cotangent):
    gathered = lax.all_gather(tokens, "row", axis=0, tiled=True)
    joined = jnp.concatenate([w_gate, w_up], axis=1)
    hidden_width = w_gate.shape[1]
    rows_in = gathered
    summed = lax.psum_scatter(
        jnp.dot(rows_in, joined, preferred_element_type=jnp.float32).astype(jnp.bfloat16),
        "col",
        scatter_dimension=0,
        tiled=True,
    ).astype(jnp.float32)
    gate_sum = summed[:, :hidden_width]
    up_sum = summed[:, hidden_width:]
    sigmoid_gate, silu_gate = gate_step(gate_sum)
    hidden_own = (silu_gate * up_sum).astype(jnp.bfloat16)
    hidden_all = lax.all_gather(hidden_own, "col", axis=0, tiled=True)
    rows_in = hidden_all
    mixed_out = lax.psum_scatter(
        jnp.dot(rows_in, w_down, preferred_element_type=jnp.float32).astype(jnp.bfloat16),
        "row",
        scatter_dimension=0,
        tiled=True,
    )
    grad_rows = lax.all_gather(cotangent, "row", axis=0, tiled=True)
    grad_down = over_tokens(hidden_all, grad_rows).astype(jnp.bfloat16)
    rows_in = grad_rows
    hidden_grad = lax.psum_scatter(
        lax.dot_general(
            rows_in, w_down, (((1,), (1,)), ((), ())), preferred_element_type=jnp.float32
        ).astype(jnp.bfloat16),
        "col",
        scatter_dimension=0,
        tiled=True,
    ).astype(jnp.float32)
    pre_gate, pre_up = backward_step(hidden_grad, gate_sum, up_sum)
    pre_gate_all, pre_up_all = (
        lax.all_gather(pre_gate, "col", axis=0, tiled=True),
        lax.all_gather(pre_up, "col", axis=0, tiled=True),
    )
    grad_gate = over_tokens(gathered, pre_gate_all).astype(jnp.bfloat16)
    grad_up = over_tokens(gathered, pre_up_all).astype(jnp.bfloat16)
    return (mixed_out, grad_gate, grad_up, grad_down)


def solution(mesh):
    return jax.shard_map(
        local,
        mesh=mesh,
        in_specs=(
            P("row", "col"),
            P("col", "row"),
            P("col", "row"),
            P("row", "col"),
            P("row", "col"),
        ),
        out_specs=(P("row", "col"), P("col", "row"), P("col", "row"), P("row", "col")),
        check_vma=False,
    )
```

profile of v0, /device:TPU:0, one launch (start us, length us, event | category | flops | bytes accessed | tf_op | source)
XLA Modules:
  0.0 475.9 jit_solution(4955347080249788818)
XLA Ops:
  7.2 0.0 all-gather.6.cloned.1.call-start
  7.2 0.7 all-gather.6.cloned.1.call-update
  7.9 0.0 all-gather.10.cloned.1.call-start
  7.9 0.7 all-gather.10.cloned.1.call-update
  8.6 0.0 reduce-scatter.4.cloned.1.call-start
  8.7 77.6 %all-gather.6.cloned.1.call-done = bf16[1024,2048]{1,0:T(8,128)(2,1)} async-done(((bf16[128,2048]{1,0:T(8,128)(2,1)}), bf16[1024,2048]{1,0:T(8,128)(2,1)}) %all-gather.6.cloned.1.call-update) | async-done | bytes 4194320 | tf_op jit(solution)/shard_map/all_gather | solution.py:28
  86.3 23.4 %fusion.9 = bf16[1024,3584]{0,1:T(8,128)(2,1)} fusion(bf16[1024,2048]{1,0:T(8,128)(2,1)} %all-gather.6.cloned.1.call-done, bf16[2048,1792]{1,0:T(8,128)(2,1)} %param.7, bf16[2048,1792]{1,0:T(8,128)(2,1)} %param.6), kind=kOutput, calls=%fused_computation.10 | convolution fusion | flops 15065415680 | bytes 26214400 | tf_op jit(solution)/shard_map/dot_general | solution.py:33
  109.7 0.0 reduce-scatter.4.cloned.1.call-update
  109.7 0.0 reduce-scatter.8.cloned.1.call-start
  109.8 50.3 %all-gather.10.cloned.1.call-done = bf16[1024,2048]{1,0:T(8,128)(2,1)} async-done(((bf16[128,2048]{1,0:T(8,128)(2,1)}), bf16[1024,2048]{1,0:T(8,128)(2,1)}) %all-gather.10.cloned.1.call-update) | async-done | bytes 4194320 | tf_op jit(solution)/shard_map/all_gather | solution.py:50
  160.1 12.5 %convolution_convert_fusion.3 = bf16[1024,1792]{0,1:T(8,128)(2,1)} fusion(bf16[1024,2048]{1,0:T(8,128)(2,1)} %all-gather.10.cloned.1.call-done, bf16[1792,2048]{1,0:T(8,128)(2,1)} %param.8), kind=kOutput, calls=%fused_computation.11 | convolution fusion | flops 7518027776 | bytes 15204352 | tf_op jit(solution)/shard_map/dot_general | solution.py:54
  172.6 0.0 reduce-scatter.8.cloned.1.call-update
  172.6 0.2 all-gather.8.cloned.1.call-start
  172.9 54.1 %reduce-scatter.4.cloned.1.call-done = bf16[256,3584]{0,1:T(8,128)(2,1)} async-done(((bf16[1024,3584]{0,1:T(8,128)(2,1)}), bf16[256,3584]{0,1:T(8,128)(2,1)}) %reduce-scatter.4.cloned.1.call-update) | async-done | bytes 1835024 | tf_op jit(solution)/shard_map/reduce_scatter | solution.py:32
  227.0 3.6 convert_element_type.44
  230.6 40.8 %reduce-scatter.8.cloned.1.call-done = bf16[256,1792]{0,1:T(8,128)(2,1)} async-done(((bf16[1024,1792]{0,1:T(8,128)(2,1)}), bf16[256,1792]{0,1:T(8,128)(2,1)}) %reduce-scatter.8.cloned.1.call-update) | async-done | bytes 917520 | tf_op jit(solution)/shard_map/reduce_scatter | solution.py:53
  271.4 5.2 %fusion.15 = (bf16[256,1792]{0,1:T(8,128)(2,1)}, bf16[256,1792]{0,1:T(8,128)(2,1)}, bf16[256,1792]{0,1:T(8,128)(2,1)}) fusion(bf16[256,1792]{0,1:T(8,128)(2,1)} %reduce-scatter.8.cloned.1.call-done, f32[256,3584]{0,1:T(8,128)} %convert_element_type.44), kind=kLoop, calls=%fused_computation.18 | loop fusion | flops 7340032 | bytes 7340032 | tf_op jit(solution)/shard_map/convert_element_type | solution.py:23
  276.6 0.0 all-gather.8.cloned.1.call-update
  276.6 0.0 all-gather.12.cloned.1.call-start
  276.7 0.5 all-gather.12.cloned.1.call-update
  277.2 0.0 all-gather.14.cloned.1.call-start
  277.3 0.7 all-gather.14.cloned.1.call-update
  278.0 0.0 reduce-scatter.6.cloned.1.call-start
  278.0 30.8 %all-gather.8.cloned.1.call-done = bf16[1024,1792]{0,1:T(8,128)(2,1)} async-done(((bf16[256,1792]{0,1:T(8,128)(2,1)}), bf16[1024,1792]{0,1:T(8,128)(2,1)}) %all-gather.8.cloned.1.call-update) | async-done | bytes 3670032 | tf_op jit(solution)/shard_map/all_gather | solution.py:42
  308.8 12.6 %convolution_convert_fusion.4 = bf16[1024,2048]{1,0:T(8,128)(2,1)} fusion(bf16[1024,1792]{0,1:T(8,128)(2,1)} %all-gather.8.cloned.1.call-done, bf16[1792,2048]{1,0:T(8,128)(2,1)} %param.8), kind=kOutput, calls=%fused_computation.12 | convolution fusion | flops 7518289920 | bytes 15204352 | tf_op jit(solution)/shard_map/dot_general | solution.py:45
  321.4 0.0 reduce-scatter.6.cloned.1.call-update
  321.4 21.3 %all-gather.12.cloned.1.call-done = bf16[1024,1792]{0,1:T(8,128)(2,1)} async-done(((bf16[256,1792]{0,1:T(8,128)(2,1)}), bf16[1024,1792]{0,1:T(8,128)(2,1)}) %all-gather.12.cloned.1.call-update) | async-done | bytes 3670032 | tf_op jit(solution)/shard_map/all_gather | solution.py:63
  342.8 12.5 %fusion.7 = bf16[2048,1792]{0,1:T(8,128)(2,1)} fusion(bf16[1024,1792]{0,1:T(8,128)(2,1)} %all-gather.12.cloned.1.call-done, bf16[1024,2048]{1,0:T(8,128)(2,1)} %all-gather.6.cloned.1.call-done), kind=kOutput, calls=%fused_computation.8 | convolution fusion | flops 7519862784 | bytes 15204352 | tf_op jit(solution)/shard_map/dot_general | solution.py:8
  355.3 10.0 %copy.10 = bf16[2048,1792]{1,0:T(8,128)(2,1)} copy(bf16[2048,1792]{0,1:T(8,128)(2,1)} %fusion.7) | data formatting | bytes 14680064
  365.2 11.7 %all-gather.14.cloned.1.call-done = bf16[1024,1792]{0,1:T(8,128)(2,1)} async-done(((bf16[256,1792]{0,1:T(8,128)(2,1)}), bf16[1024,1792]{0,1:T(8,128)(2,1)}) %all-gather.14.cloned.1.call-update) | async-done | bytes 3670032 | tf_op jit(solution)/shard_map/all_gather | solution.py:64
  376.9 12.5 %fusion.8 = bf16[2048,1792]{0,1:T(8,128)(2,1)} fusion(bf16[1024,1792]{0,1:T(8,128)(2,1)} %all-gather.14.cloned.1.call-done, bf16[1024,2048]{1,0:T(8,128)(2,1)} %all-gather.6.cloned.1.call-done), kind=kOutput, calls=%fused_computation.9 | convolution fusion | flops 7519862784 | bytes 15204352 | tf_op jit(solution)/shard_map/dot_general | solution.py:8
  389.4 9.9 %copy.11 = bf16[2048,1792]{1,0:T(8,128)(2,1)} copy(bf16[2048,1792]{0,1:T(8,128)(2,1)} %fusion.8) | data formatting | bytes 14680064
  399.4 12.6 %convolution_convert_fusion = bf16[1792,2048]{1,0:T(8,128)(2,1)} fusion(bf16[1024,1792]{0,1:T(8,128)(2,1)} %all-gather.8.cloned.1.call-done, bf16[1024,2048]{1,0:T(8,128)(2,1)} %all-gather.10.cloned.1.call-done), kind=kOutput, calls=%fused_computation.5 | convolution fusion | flops 7519862784 | bytes 15204352 | tf_op jit(solution)/shard_map/dot_general | solution.py:8
  411.9 57.1 %reduce-scatter.6.cloned.1.call-done = bf16[128,2048]{1,0:T(8,128)(2,1)} async-done(((bf16[1024,2048]{1,0:T(8,128)(2,1)}), bf16[128,2048]{1,0:T(8,128)(2,1)}) %reduce-scatter.6.cloned.1.call-update) | async-done | bytes 524304 | tf_op jit(solution)/shard_map/reduce_scatter | solution.py:44
Async XLA Ops:
  7.2 79.1 %all-gather.6.cloned.1.call-start = ((), (), s32[]{:S(2)}) async-start(), calls=%async_computation.3 | async-start | bytes 4718592 | tf_op jit(solution)/shard_map/all_gather | solution.py:28
  7.9 152.2 %all-gather.10.cloned.1.call-start = ((), (), s32[]{:S(2)}) async-start(), calls=%async_computation.7 | async-start | bytes 4718592 | tf_op jit(solution)/shard_map/all_gather | solution.py:50
  8.6 218.3 %reduce-scatter.4.cloned.1.call-start = ((), (), s32[]{:S(2)}) async-start(), calls=%async_computation.4 | async-start | bytes 9175040 | tf_op jit(solution)/shard_map/reduce_scatter | solution.py:32
  109.7 161.7 %reduce-scatter.8.cloned.1.call-start = ((), (), s32[]{:S(2)}) async-start(), calls=%async_computation.8 | async-start | bytes 4587520 | tf_op jit(solution)/shard_map/reduce_scatter | solution.py:53
  172.6 136.1 %all-gather.8.cloned.1.call-start = ((), (), s32[]{:S(2)}) async-start(), calls=%async_computation.5 | async-start | bytes 4587520 | tf_op jit(solution)/shard_map/all_gather | solution.py:42
  276.6 66.1 %all-gather.12.cloned.1.call-start = ((), (), s32[]{:S(2)}) async-start(), calls=%async_computation.9 | async-start | bytes 4587520 | tf_op jit(solution)/shard_map/all_gather | solution.py:63
  277.2 99.7 %all-gather.14.cloned.1.call-start = ((), (), s32[]{:S(2)}) async-start(), calls=%async_computation.10 | async-start | bytes 4587520 | tf_op jit(solution)/shard_map/all_gather | solution.py:64
  278.0 191.1 %reduce-scatter.6.cloned.1.call-start = ((), (), s32[]{:S(2)}) async-start(), calls=%async_computation.6 | async-start | bytes 4718592 | tf_op jit(solution)/shard_map/reduce_scatter | solution.py:44
Sparse Core Ops, SparseCore 0:
  10.1 76.0 all-gather.5
  88.4 71.6 all-gather.9
  163.2 63.7 reduce-scatter.3
  230.1 41.2 reduce-scatter.7
  276.8 31.9 all-gather.7
  310.8 31.9 all-gather.11
  344.9 31.9 all-gather.13
  381.1 87.9 reduce-scatter.5
where the time goes:
time: 476 us
  waiting for transfers between devices  346 us (73%)
  matrix products  86.2 us (18%)
  local copies, waits for them, and re-layouts  19.9 us (4%)
  between operations  14.1 us (3%)
  other arithmetic  8.86 us (2%)
    all_gather x1, waiting for transfers between devices, local(): gathered = lax.all_gather(tokens, 'row', axis=0, tiled=True)  77.6 us
    reduce_scatter x1, waiting for transfers between devices, local(): lax.psum_scatter(jnp.dot(rows_in, w_down, preferred_element_type=jnp.floa...  57.1 us
    reduce_scatter x1, waiting for transfers between devices, local(): lax.psum_scatter(jnp.dot(rows_in, joined, preferred_element_type=jnp.floa...  54.1 us
    all_gather x1, waiting for transfers between devices, local(): grad_rows = lax.all_gather(cotangent, 'row', axis=0, tiled=True)  50.3 us
    reduce_scatter x1, waiting for transfers between devices, local(): lax.psum_scatter(lax.dot_general(rows_in, w_down, (((1,), (1,)), ((), ())...  40.8 us
    dot_general x3, matrix products, over_tokens(): lax.dot_general(left, right, (((0,), (0,)), ((), ())), preferred_element_...  37.6 us
    all_gather x1, waiting for transfers between devices, local(): hidden_all = lax.all_gather(hidden_own, 'col', axis=0, tiled=True)  30.8 us
    dot_general x1, matrix products, local(): jnp.dot(rows_in, joined, preferred_element_type=jnp.float32)  23.4 us
  transfers between devices with their start and end apart: 8, of which 8 were waited for; matrix products, arithmetic and copies ran while one was open for 23% of the time, Pallas kernels for 0%

commit v1 on v0

v1 whole, which is shorter than its diff:
```python
import functools

import jax
import jax.numpy as jnp
from jax import lax
from jax.experimental import pallas as pl
from jax.experimental.pallas import tpu as pltpu
from jax.sharding import PartitionSpec as P

MESH = pl.DeviceIdType.MESH
F32 = jnp.float32
BF16 = jnp.bfloat16
Z = 4
LAG = 3


def over_tokens(left, right):
    return lax.dot_general(
        left, right, (((0,), (0,)), ((), ())), preferred_element_type=F32
    )


def nearest(at, k, n):
    other = n - 1 - at
    low = jnp.where(at <= other, at, other)
    half = (k + 1) // 2
    near = jnp.where(k % 2 == 1, at + half, at - half)
    far = jnp.where(at <= other, k, n - 1 - k)
    return jnp.where(k <= 2 * low, near, far)


def gather_kernel(
    n_row, n_col, tile,
    tok_ref, wg_ref, wu_ref, wd_ref, cot_ref,
    tok_out, cot_out, act_out,
    tok_all, cot_all, wg, wu, wd, part, pair_in, pair_sum, x_in,
    load_sem, tok_recv, cot_recv, tok_send, cot_send, keep_sem,
    pair_send, pair_recv, x_send, x_recv, act_keep, act_send, act_recv,
):
    n_y = n_row // Z
    n_x = n_col // 2
    row = lax.axis_index("row")
    col = lax.axis_index("col")
    z, y = row // n_y, row % n_y
    x, core = col // 2, col % 2
    twin = x * 2 + 1 - core
    rows = tok_ref.shape[0]
    half = rows // 2
    width = wg_ref.shape[1]
    own = pl.multiple_of(core * half, half)
    away = pl.multiple_of((1 - core) * half, half)

    loads = [
        pltpu.make_async_copy(tok_ref, tok_all.at[row], load_sem.at[0]),
        pltpu.make_async_copy(cot_ref, cot_all.at[row], load_sem.at[1]),
        pltpu.make_async_copy(wg_ref, wg, load_sem.at[2]),
        pltpu.make_async_copy(wu_ref, wu, load_sem.at[3]),
        pltpu.make_async_copy(wd_ref, wd, load_sem.at[4]),
    ]
    for load in loads:
        load.start()

    barrier = pltpu.get_barrier_semaphore()
    sides = (
        (z < Z - 1, row + n_y),
        (z > 0, row - n_y),
        (y < n_y - 1, row + 1),
        (y > 0, row - 1),
    )
    for there, who in sides:
        @pl.when(there)
        def _():
            pl.semaphore_signal(barrier, inc=1, device_id=(who, col), device_id_type=MESH)
    pl.semaphore_signal(barrier, inc=1, device_id=(row, twin), device_id_type=MESH)
    for k in range(1, n_x):
        peer = ((x + k) % n_x) * 2 + core
        pl.semaphore_signal(barrier, inc=1, device_id=(row, peer), device_id_type=MESH)
    peers = jnp.int32(n_x)
    for there, _ in sides:
        peers = peers + there.astype(jnp.int32)
    pl.semaphore_wait(barrier, peers)

    def shard(i):
        return nearest(z, i // n_y, Z) * n_y + nearest(y, i % n_y, n_y)

    def forwards(o, buf, send, recv):
        zo, yo = o // n_y, o % n_y
        whens = (
            (yo == y) & (z >= zo) & (z < Z - 1),
            (yo == y) & (z <= zo) & (z > 0),
            (y >= yo) & (y < n_y - 1),
            (y <= yo) & (y > 0),
        )
        out = []
        for d, (when, (_, who)) in enumerate(zip(whens, sides)):
            out.append((when, pltpu.make_async_remote_copy(
                src_ref=buf.at[o], dst_ref=buf.at[o],
                send_sem=send.at[o, d], recv_sem=recv.at[o],
                device_id=(who, col), device_id_type=MESH,
            )))
        return out

    def arrived(o, buf, send, recv):
        pltpu.make_async_remote_copy(
            src_ref=buf.at[o], dst_ref=buf.at[o],
            send_sem=send.at[o, 0], recv_sem=recv.at[o],
            device_id=(row, twin), device_id_type=MESH,
        ).wait_recv()

    def pair_copy(o, slot):
        return pltpu.make_async_remote_copy(
            src_ref=part.at[slot, :, pl.ds(away, half)], dst_ref=pair_in.at[o],
            send_sem=pair_send.at[o], recv_sem=pair_recv.at[o],
            device_id=(row, twin), device_id_type=MESH,
        )

    def x_copy(o, k):
        peer = ((x + k) % n_x) * 2 + core
        return pltpu.make_async_remote_copy(
            src_ref=pair_sum.at[o], dst_ref=x_in.at[o, k - 1],
            send_sem=x_send.at[o, k - 1], recv_sem=x_recv.at[o, k - 1],
            device_id=(row, peer), device_id_type=MESH,
        )

    def act_rows(o):
        return act_out.at[:, pl.ds(pl.multiple_of(o * rows + core * half, half), half)]

    def act_rows_in(o):
        return act_out.at[:, pl.ds(pl.multiple_of(o * rows + (1 - core) * half, half), half)]

    def act_local(o):
        return pltpu.make_async_copy(x_in.at[o, 0], act_rows(o), act_keep.at[o])

    def act_copy(o):
        return pltpu.make_async_remote_copy(
            src_ref=x_in.at[o, 0], dst_ref=act_rows(o),
            send_sem=act_send.at[o], recv_sem=act_recv.at[o],
            device_id=(row, twin), device_id_type=MESH,
        )

    def act_arrival(o):
        return pltpu.make_async_remote_copy(
            src_ref=x_in.at[o, 0], dst_ref=act_rows_in(o),
            send_sem=act_send.at[o], recv_sem=act_recv.at[o],
            device_id=(row, twin), device_id_type=MESH,
        )

    def keeps(o):
        to = pl.ds(pl.multiple_of(o * rows, rows), rows)
        return (
            pltpu.make_async_copy(tok_all.at[o], tok_out.at[to], keep_sem.at[o, 0]),
            pltpu.make_async_copy(cot_all.at[o], cot_out.at[to], keep_sem.at[o, 1]),
        )

    def start_forwards(o, buf, send, recv):
        for when, copy in forwards(o, buf, send, recv):
            @pl.when(when)
            def _():
                copy.start()

    def sum_pair(i):
        o, slot = shard(i), i % 2
        copy = pair_copy(o, slot)
        copy.wait()

        @pl.loop(0, width // tile)
        def _(t):
            cols = pl.ds(pl.multiple_of(t * tile, tile), tile)
            for a in range(3):
                pair_sum[o, a, :, cols] = (
                    part[slot, a, pl.ds(own, half), cols].astype(F32)
                    + pair_in[o, a, :, cols].astype(F32)
                ).astype(BF16)

        for k in range(1, n_x):
            x_copy(o, k).start()

    def finish(i):
        o = shard(i)
        for k in range(1, n_x):
            x_copy(o, k).wait_recv()

        @pl.loop(0, width // tile)
        def _(t):
            cols = pl.ds(pl.multiple_of(t * tile, tile), tile)

            def total(a):
                v = pair_sum[o, a, :, cols].astype(F32)
                for k in range(n_x - 1):
                    v = v + x_in[o, k, a, :, cols].astype(F32)
                return v

            gate, up, grad = total(0), total(1), total(2)
            s = jax.nn.sigmoid(gate)
            silu = gate * s
            x_in[o, 0, 0, :, cols] = (silu * up).astype(BF16)
            x_in[o, 0, 1, :, cols] = (grad * up * s * (1.0 + gate * (1.0 - s))).astype(BF16)
            x_in[o, 0, 2, :, cols] = (grad * silu).astype(BF16)

        act_local(o).start()
        act_copy(o).start()

    def step(i, carry):
        o = shard(i)

        @pl.when(i == 0)
        def _():
            loads[0].wait()

        @pl.when(i > 0)
        def _():
            arrived(o, tok_all, tok_send, tok_recv)

        start_forwards(o, tok_all, tok_send, tok_recv)

        @pl.when(i == 0)
        def _():
            loads[1].wait()

        @pl.when(i > 0)
        def _():
            arrived(o, cot_all, cot_send, cot_recv)

        start_forwards(o, cot_all, cot_send, cot_recv)
        for keep in keeps(o):
            keep.start()

        @pl.when(i == 0)
        def _():
            for load in loads[2:]:
                load.wait()

        slot = i % 2

        @pl.loop(0, width // tile)
        def _(t):
            cols = pl.ds(pl.multiple_of(t * tile, tile), tile)
            part[slot, 0, :, cols] = jnp.dot(
                tok_all[o], wg[:, cols], preferred_element_type=F32).astype(BF16)
            part[slot, 1, :, cols] = jnp.dot(
                tok_all[o], wu[:, cols], preferred_element_type=F32).astype(BF16)
            part[slot, 2, :, cols] = lax.dot_general(
                cot_all[o], wd[cols, :], (((1,), (1,)), ((), ())),
                preferred_element_type=F32).astype(BF16)

        pair_copy(o, slot).start()

        @pl.when(i > 0)
        def _():
            sum_pair(i - 1)

        @pl.when(i >= LAG)
        def _():
            finish(i - LAG)

        return carry

    lax.fori_loop(0, n_row, step, 0)
    sum_pair(n_row - 1)

    def rest(i, carry):
        finish(i)
        return carry

    lax.fori_loop(n_row - LAG, n_row, rest, 0)

    def drain(o, carry):
        for buf, send, recv in ((tok_all, tok_send, tok_recv), (cot_all, cot_send, cot_recv)):
            for when, copy in forwards(o, buf, send, recv):
                @pl.when(when)
                def _():
                    copy.wait_send()
        for keep in keeps(o):
            keep.wait()
        for k in range(1, n_x):
            x_copy(o, k).wait_send()
        act_local(o).wait()
        act_copy(o).wait_send()
        act_arrival(o).wait_recv()
        return carry

    lax.fori_loop(0, n_row, drain, 0)


def gather_and_act(n_row, n_col, tokens, w_gate, w_up, w_down, cotangent):
    rows, depth = tokens.shape
    width = w_gate.shape[1]
    half = rows // 2
    n_x = n_col // 2
    tile = 256 if width % 256 == 0 else 128
    dma = pltpu.SemaphoreType.DMA
    flops = 2 * n_row * rows * depth * width * 3
    return pl.pallas_call(
        functools.partial(gather_kernel, n_row, n_col, tile),
        out_shape=(
            jax.ShapeDtypeStruct((n_row * rows, depth), BF16),
            jax.ShapeDtypeStruct((n_row * rows, depth), BF16),
            jax.ShapeDtypeStruct((3, n_row * rows, width), BF16),
        ),
        in_specs=[pl.BlockSpec(memory_space=pl.ANY)] * 5,
        out_specs=[pl.BlockSpec(memory_space=pl.ANY)] * 3,
        scratch_shapes=[
            pltpu.VMEM((n_row, rows, depth), BF16),
            pltpu.VMEM((n_row, rows, depth), BF16),
            pltpu.VMEM((depth, width), BF16),
            pltpu.VMEM((depth, width), BF16),
            pltpu.VMEM((width, depth), BF16),
            pltpu.VMEM((2, 3, rows, width), BF16),
            pltpu.VMEM((n_row, 3, half, width), BF16),
            pltpu.VMEM((n_row, 3, half, width), BF16),
            pltpu.VMEM((n_row, n_x - 1, 3, half, width), BF16),
            dma((5,)),
            dma((n_row,)),
            dma((n_row,)),
            dma((n_row, 4)),
            dma((n_row, 4)),
            dma((n_row, 2)),
            dma((n_row,)),
            dma((n_row,)),
            dma((n_row, n_x - 1)),
            dma((n_row, n_x - 1)),
            dma((n_row,)),
            dma((n_row,)),
            dma((n_row,)),
        ],
        compiler_params=pltpu.CompilerParams(
            collective_id=0, has_side_effects=True, vmem_limit_bytes=60 * 1024 * 1024
        ),
        cost_estimate=pl.CostEstimate(
            flops=flops, bytes_accessed=6 * depth * width, transcendentals=0
        ),
    )(tokens, w_gate, w_up, w_down, cotangent)


def local(n_row, n_col, tokens, w_gate, w_up, w_down, cotangent):
    gathered, grad_rows, act = gather_and_act(
        n_row, n_col, tokens, w_gate, w_up, w_down, cotangent)
    hidden, pre_gate, pre_up = act[0], act[1], act[2]
    mixed_out = lax.psum_scatter(
        jnp.dot(hidden, w_down, preferred_element_type=F32).astype(BF16),
        "row",
        scatter_dimension=0,
        tiled=True,
    )
    grad_down = over_tokens(hidden, grad_rows).astype(BF16)
    grad_gate = over_tokens(gathered, pre_gate).astype(BF16)
    grad_up = over_tokens(gathered, pre_up).astype(BF16)
    return (mixed_out, grad_gate, grad_up, grad_down)


def solution(mesh):
    n_row, n_col = mesh.shape["row"], mesh.shape["col"]
    return jax.shard_map(
        functools.partial(local, n_row, n_col),
        mesh=mesh,
        in_specs=(
            P("row", "col"),
            P("col", "row"),
            P("col", "row"),
            P("row", "col"),
            P("row", "col"),
        ),
        out_specs=(P("row", "col"), P("col", "row"), P("col", "row"), P("row", "col")),
        check_vma=False,
    )
```

time: 476 us -> 283 us (0.59)
  waiting for transfers between devices: 346 us -> 55.8 us
  Pallas kernels: 0 us -> 167 us
  matrix products: 86.2 us -> 45.9 us
  local copies, waits for them, and re-layouts: 19.9 us -> 0.02 us
  other arithmetic: 8.86 us -> 0.01 us
    all_gather x5 -> x0, waiting for transfers between devices: 192 us -> none  [the longest x1 77.6 us: local(): gathered = lax.all_gather(tokens, 'row', axis=0, tiled=True)]
    pallas_call x0 -> x1, Pallas kernels: none -> 167 us  [gather_and_act(): pl.pallas_call(functools.partial(gather_kernel, n_row, n_col, tile), out_...]
    reduce_scatter x3 -> x1, waiting for transfers between devices: 152 us -> 55.8 us  [local(): lax.psum_scatter(jnp.dot(hidden, w_down, preferred_element_type=F32).asty...]
    dot_general x3 -> x1, matrix products: 48.6 us -> 13 us  [local(): jnp.dot(hidden, w_down, preferred_element_type=F32).astype(BF16)]
    unnamed x2 -> x10, local copies, waits for them, and re-layouts: 19.9 us -> 0.02 us
    convert_element_type x2 -> x0, other arithmetic: 8.86 us -> none  [the longest x1 5.24 us: backward_step(): pre_up = (hidden_grad * silu_gate).astype(jnp.bfloat16)]
  transfers between devices with their start and end apart: 8 -> 1, of which waited for: 8 -> 1; matrix products, arithmetic and copies ran while one was open for 23% -> 12% of each run, Pallas kernels for 0% -> 0%
where the time goes in v1:
time: 283 us
  Pallas kernels  167 us (59%)
  waiting for transfers between devices  55.8 us (20%)
  matrix products  45.9 us (16%)
  between operations  14.1 us (5%)
    pallas_call x1, Pallas kernels, gather_and_act(): pl.pallas_call(functools.partial(gather_kernel, n_row, n_col, tile), out_...  167 us
    reduce_scatter x1, waiting for transfers between devices, local(): lax.psum_scatter(jnp.dot(hidden, w_down, preferred_element_type=F32).asty...  55.8 us
    dot_general x3, matrix products, over_tokens(): lax.dot_general(left, right, (((0,), (0,)), ((), ())), preferred_element_...  33 us
    dot_general x1, matrix products, local(): jnp.dot(hidden, w_down, preferred_element_type=F32).astype(BF16)  13 us
  transfers between devices with their start and end apart: 1, of which 1 were waited for; matrix products, arithmetic and copies ran while one was open for 12% of the time, Pallas kernels for 0%

profile of v1, /device:TPU:0, one launch (start us, length us, event | category | flops | bytes accessed | tf_op | source)
XLA Modules:
  0.0 283.3 jit_solution(7189463089476189347)
XLA Ops:
  7.2 0.0 reduce-scatter.2.cloned.1.call-start
  7.2 167.5 %shard_map.84 = (bf16[1024,2048]{1,0:T(8,128)(2,1)}, bf16[1024,2048]{1,0:T(8,128)(2,1)}, bf16[3,1024,1792]{2,1,0:T(8,128)(2,1)}) custom-call(bf16[128,2048]{1,0:T(8,128)(2,1)} %tok_ref.1, bf16[2048,1792]{1,0:T(8,128)(2,1)} %wg_ref.1, bf16[2048,1792]{1,0:T(8,128)(2,1)} %wu_ref.1, bf16[1792,2048]{1,0:T(8,128)(2,1)} %wd_ref.1, bf16[128,2048]{1,0:T(8,128)(2,1)} %cot_ref.1), custom_call_target="tpu_custom_call" | custom-call | flops 22548578304 | bytes 22020096 | tf_op jit(solution)/shard_map/pallas_call | solution.py:293
  174.7 13.0 %convolution_convert_fusion.3 = bf16[1024,2048]{1,0:T(8,128)(2,1)} fusion(bf16[1792,2048]{1,0:T(8,128)(2,1)} %wd_ref.1, bf16[3,1024,1792]{2,1,0:T(8,128)(2,1)} %get-tuple-element.7), kind=kOutput, calls=%fused_computation.3 | convolution fusion | flops 7518289920 | bytes 15204352 | tf_op jit(solution)/shard_map/dot_general | solution.py:340
  187.7 0.0 slice-start
  187.7 0.0 reduce-scatter.2.cloned.1.call-update
  187.7 0.0 slice-start.1
  187.7 0.0 slice-start.2
  187.7 0.0 copy-start
  187.7 12.8 %convolution_convert_fusion.1 = bf16[2048,1792]{1,0:T(8,128)(2,1)} fusion(bf16[1024,2048]{1,0:T(8,128)(2,1)} %get-tuple-element.8, bf16[3,1024,1792]{2,1,0:T(8,128)(2,1)} %get-tuple-element.7), kind=kOutput, calls=%fused_computation.1 | convolution fusion | flops 7519862784 | bytes 15204352 | tf_op jit(solution)/shard_map/dot_general | solution.py:18
  200.5 0.0 slice-done
  200.5 0.0 slice-done.1
  200.5 0.0 slice-done.2
  200.5 0.0 copy-done
  200.5 0.0 copy-start.1
  200.5 10.1 %convolution_convert_fusion.2 = bf16[2048,1792]{1,0:T(8,128)(2,1)} fusion(bf16[1024,2048]{1,0:T(8,128)(2,1)S(1)} %copy-done, bf16[3,1024,1792]{2,1,0:T(8,128)(2,1)S(1)} %bitcast.16), kind=kOutput, calls=%fused_computation.2 | convolution fusion | flops 7519862784 | bytes 15204352 | tf_op jit(solution)/shard_map/dot_general | solution.py:18
  210.6 0.0 copy-done.1
  210.6 10.1 %convolution_convert_fusion = bf16[1792,2048]{1,0:T(8,128)(2,1)} fusion(bf16[1024,2048]{1,0:T(8,128)(2,1)S(1)} %copy-done.1, bf16[3,1024,1792]{2,1,0:T(8,128)(2,1)S(1)} %bitcast.16), kind=kOutput, calls=%fused_computation | convolution fusion | flops 7519862784 | bytes 15204352 | tf_op jit(solution)/shard_map/dot_general | solution.py:18
  220.7 55.8 %reduce-scatter.2.cloned.1.call-done = bf16[128,2048]{1,0:T(8,128)(2,1)} async-done(((bf16[1024,2048]{1,0:T(8,128)(2,1)}), bf16[128,2048]{1,0:T(8,128)(2,1)}) %reduce-scatter.2.cloned.1.call-update) | async-done | bytes 524304 | tf_op jit(solution)/shard_map/reduce_scatter | solution.py:339
  (1 shorter events, 0.0 us)
Async XLA Ops:
  7.2 269.3 %reduce-scatter.2.cloned.1.call-start = ((), (), s32[]{:S(2)}) async-start(), calls=%async_computation.1 | async-start | bytes 4718592 | tf_op jit(solution)/shard_map/reduce_scatter | solution.py:339
  187.7 12.8 %slice-start = ((s8[11010048]{0:T(1024)(128)(4,1)}), s8[2621440]{0:T(1024)(128)(4,1)S(1)}, s32[]{:S(2)}) async-start(s8[11010048]{0:T(1024)(128)(4,1)} %bitcast.15), calls=%async_computation.2 | async-start | bytes 5242880
  187.7 12.8 %slice-start.1 = ((s8[11010048]{0:T(1024)(128)(4,1)}), s8[4194304]{0:T(1024)(128)(4,1)S(1)}, s32[]{:S(2)}) async-start(s8[11010048]{0:T(1024)(128)(4,1)} %bitcast.15), calls=%async_computation.3 | async-start | bytes 8388608
  187.7 12.8 %slice-start.2 = ((s8[11010048]{0:T(1024)(128)(4,1)}), s8[4194304]{0:T(1024)(128)(4,1)S(1)}, s32[]{:S(2)}) async-start(s8[11010048]{0:T(1024)(128)(4,1)} %bitcast.15), calls=%async_computation.4 | async-start | bytes 8388608
  187.7 12.8 %copy-start = (bf16[1024,2048]{1,0:T(8,128)(2,1)S(1)}, bf16[1024,2048]{1,0:T(8,128)(2,1)}, u32[]{:S(2)}) copy-start(bf16[1024,2048]{1,0:T(8,128)(2,1)} %get-tuple-element.8) | copy-start | bytes 12582916
  200.5 10.1 %copy-start.1 = (bf16[1024,2048]{1,0:T(8,128)(2,1)S(1)}, bf16[1024,2048]{1,0:T(8,128)(2,1)}, u32[]{:S(2)}) copy-start(bf16[1024,2048]{1,0:T(8,128)(2,1)} %get-tuple-element.9) | copy-start | bytes 12582916
Sparse Core Ops, SparseCore 0:
  187.8 88.6 reduce-scatter.1

commit v2 on v0

v2 whole, which is shorter than its diff:
```python
import functools

import jax
import jax.numpy as jnp
from jax import lax
from jax.experimental import pallas as pl
from jax.experimental.pallas import tpu as pltpu
from jax.sharding import PartitionSpec as P

MESH = pl.DeviceIdType.MESH
F32 = jnp.float32
BF16 = jnp.bfloat16
Z = 4
LAG = 3
CLOSE = 3


def over_tokens(left, right):
    return lax.dot_general(
        left, right, (((0,), (0,)), ((), ())), preferred_element_type=F32
    )


def nearest(at, k, n):
    other = n - 1 - at
    low = jnp.where(at <= other, at, other)
    half = (k + 1) // 2
    near = jnp.where(k % 2 == 1, at + half, at - half)
    far = jnp.where(at <= other, k, n - 1 - k)
    return jnp.where(k <= 2 * low, near, far)


class Place:
    def __init__(self, n_row, n_col):
        self.n_y = n_row // Z
        self.n_x = n_col // 2
        self.row = lax.axis_index("row")
        self.col = lax.axis_index("col")
        self.z, self.y = self.row // self.n_y, self.row % self.n_y
        self.x, self.core = self.col // 2, self.col % 2
        self.twin = self.x * 2 + 1 - self.core
        self.sides = (
            (self.z < Z - 1, self.row + self.n_y),
            (self.z > 0, self.row - self.n_y),
            (self.y < self.n_y - 1, self.row + 1),
            (self.y > 0, self.row - 1),
        )

    def peer(self, k):
        return ((self.x + k) % self.n_x) * 2 + self.core

    def greet(self, with_rows):
        barrier = pltpu.get_barrier_semaphore()
        peers = jnp.int32(self.n_x)
        if with_rows:
            for there, who in self.sides:
                peers = peers + there.astype(jnp.int32)

                @pl.when(there)
                def _():
                    pl.semaphore_signal(
                        barrier, inc=1, device_id=(who, self.col), device_id_type=MESH)
        pl.semaphore_signal(
            barrier, inc=1, device_id=(self.row, self.twin), device_id_type=MESH)
        for k in range(1, self.n_x):
            pl.semaphore_signal(
                barrier, inc=1, device_id=(self.row, self.peer(k)), device_id_type=MESH)
        pl.semaphore_wait(barrier, peers)

    def forwards(self, o, buf, send, recv):
        zo, yo = o // self.n_y, o % self.n_y
        whens = (
            (yo == self.y) & (self.z >= zo) & (self.z < Z - 1),
            (yo == self.y) & (self.z <= zo) & (self.z > 0),
            (self.y >= yo) & (self.y < self.n_y - 1),
            (self.y <= yo) & (self.y > 0),
        )
        out = []
        for d, (when, (_, who)) in enumerate(zip(whens, self.sides)):
            out.append((when, pltpu.make_async_remote_copy(
                src_ref=buf.at[o], dst_ref=buf.at[o],
                send_sem=send.at[o, d], recv_sem=recv.at[o],
                device_id=(who, self.col), device_id_type=MESH,
            )))
        return out

    def start_forwards(self, *args):
        for when, copy in self.forwards(*args):
            @pl.when(when)
            def _():
                copy.start()

    def end_forwards(self, *args):
        for when, copy in self.forwards(*args):
            @pl.when(when)
            def _():
                copy.wait_send()

    def arrived(self, o, buf, send, recv):
        pltpu.make_async_remote_copy(
            src_ref=buf.at[o], dst_ref=buf.at[o],
            send_sem=send.at[o, 0], recv_sem=recv.at[o],
            device_id=(self.row, self.twin), device_id_type=MESH,
        ).wait_recv()


class Sums:
    def __init__(self, at, tile, n_parts, part, pair_in, pair_sum, x_in,
                 pair_send, pair_recv, x_send, x_recv):
        self.at, self.tile, self.n_parts = at, tile, n_parts
        self.part, self.pair_in, self.pair_sum, self.x_in = part, pair_in, pair_sum, x_in
        self.pair_send, self.pair_recv = pair_send, pair_recv
        self.x_send, self.x_recv = x_send, x_recv
        self.half = part.shape[2] // 2
        self.width = part.shape[3]
        self.own = pl.multiple_of(at.core * self.half, self.half)
        self.away = pl.multiple_of((1 - at.core) * self.half, self.half)

    def pair_copy(self, o, slot):
        return pltpu.make_async_remote_copy(
            src_ref=self.part.at[slot, :, pl.ds(self.away, self.half)],
            dst_ref=self.pair_in.at[o],
            send_sem=self.pair_send.at[o], recv_sem=self.pair_recv.at[o],
            device_id=(self.at.row, self.at.twin), device_id_type=MESH,
        )

    def x_copy(self, o, k):
        return pltpu.make_async_remote_copy(
            src_ref=self.pair_sum.at[o], dst_ref=self.x_in.at[o, k - 1],
            send_sem=self.x_send.at[o, k - 1], recv_sem=self.x_recv.at[o, k - 1],
            device_id=(self.at.row, self.at.peer(k)), device_id_type=MESH,
        )

    def sum_pair(self, o, slot):
        self.pair_copy(o, slot).wait()

        @pl.loop(0, self.width // self.tile)
        def _(t):
            cols = pl.ds(pl.multiple_of(t * self.tile, self.tile), self.tile)
            for a in range(self.n_parts):
                self.pair_sum[o, a, :, cols] = (
                    self.part[slot, a, pl.ds(self.own, self.half), cols].astype(F32)
                    + self.pair_in[o, a, :, cols].astype(F32)
                ).astype(BF16)

        for k in range(1, self.at.n_x):
            self.x_copy(o, k).start()

    def arrive(self, o):
        for k in range(1, self.at.n_x):
            self.x_copy(o, k).wait_recv()

    def total(self, o, a, cols):
        v = self.pair_sum[o, a, :, cols].astype(F32)
        for k in range(self.at.n_x - 1):
            v = v + self.x_in[o, k, a, :, cols].astype(F32)
        return v

    def end(self, o):
        for k in range(1, self.at.n_x):
            self.x_copy(o, k).wait_send()


class Shares:
    def __init__(self, at, rows, source, place, keep, send, recv):
        self.at, self.rows, self.half = at, rows, rows // 2
        self.source, self.place = source, place
        self.keep, self.send, self.recv = keep, send, recv

    def spot(self, o, core):
        return self.place(
            pl.ds(pl.multiple_of(o * self.rows + core * self.half, self.half), self.half))

    def local(self, o):
        return pltpu.make_async_copy(
            self.source(o), self.spot(o, self.at.core), self.keep.at[o])

    def away(self, o, core):
        return pltpu.make_async_remote_copy(
            src_ref=self.source(o), dst_ref=self.spot(o, core),
            send_sem=self.send.at[o], recv_sem=self.recv.at[o],
            device_id=(self.at.row, self.at.twin), device_id_type=MESH,
        )

    def start(self, o):
        self.local(o).start()
        self.away(o, self.at.core).start()

    def end(self, o):
        self.local(o).wait()
        self.away(o, self.at.core).wait_send()
        self.away(o, 1 - self.at.core).wait_recv()


def forward_kernel(
    n_row, n_col, tile,
    tok_ref, wg_ref, wu_ref, cot_ref,
    tok_out, cot_out, hid_out, fac_out,
    tok_all, wg, wu, part, pair_in, pair_sum, x_in, fac,
    load_sem, tok_recv, cot_recv, tok_send, cot_send, keep_sem, fac_sem,
    pair_send, pair_recv, x_send, x_recv, act_keep, act_send, act_recv,
):
    at = Place(n_row, n_col)
    rows = tok_ref.shape[0]
    width = wg_ref.shape[1]

    loads = [
        pltpu.make_async_copy(tok_ref, tok_all.at[at.row], load_sem.at[0]),
        pltpu.make_async_copy(wg_ref, wg, load_sem.at[1]),
        pltpu.make_async_copy(wu_ref, wu, load_sem.at[2]),
        pltpu.make_async_copy(cot_ref, cot_out.at[at.row], load_sem.at[3]),
    ]
    for load in loads:
        load.start()
    at.greet(True)

    sums = Sums(at, tile, 2, part, pair_in, pair_sum, x_in,
                pair_send, pair_recv, x_send, x_recv)
    shares = Shares(at, rows, lambda o: x_in.at[o, 0, 0], lambda to: hid_out.at[to],
                    act_keep, act_send, act_recv)
    tok = (tok_all, tok_send, tok_recv)
    cot = (cot_out, cot_send, cot_recv)

    def shard(i):
        return nearest(at.z, i // at.n_y, Z) * at.n_y + nearest(at.y, i % at.n_y, at.n_y)

    def keep(o):
        to = pl.ds(pl.multiple_of(o * rows, rows), rows)
        return pltpu.make_async_copy(tok_all.at[o], tok_out.at[to], keep_sem.at[o])

    def fac_copy(o):
        return pltpu.make_async_copy(fac.at[o], fac_out.at[o], fac_sem.at[o])

    def finish(i):
        o = shard(i)
        sums.arrive(o)

        @pl.loop(0, width // tile)
        def _(t):
            cols = pl.ds(pl.multiple_of(t * tile, tile), tile)
            gate, up = sums.total(o, 0, cols), sums.total(o, 1, cols)
            s = jax.nn.sigmoid(gate)
            silu = gate * s
            x_in[o, 0, 0, :, cols] = (silu * up).astype(BF16)
            fac[o, 0, :, cols] = up * s * (1.0 + gate * (1.0 - s))
            fac[o, 1, :, cols] = silu

        shares.start(o)
        fac_copy(o).start()

    def step(i, carry):
        @pl.when(i > 0)
        def _():
            sums.sum_pair(shard(i - 1), (i - 1) % 2)

        o = shard(i)

        @pl.when(i == 0)
        def _():
            loads[0].wait()

        @pl.when(i > 0)
        def _():
            at.arrived(o, *tok)

        at.start_forwards(o, *tok)
        keep(o).start()

        @pl.when(i == n_row // 2)
        def _():
            loads[3].wait()
            at.start_forwards(at.row, *cot)

        @pl.when(i == 0)
        def _():
            loads[1].wait()
            loads[2].wait()

        slot = i % 2

        @pl.loop(0, width // tile)
        def _(t):
            cols = pl.ds(pl.multiple_of(t * tile, tile), tile)
            part[slot, 0, :, cols] = jnp.dot(
                tok_all[o], wg[:, cols], preferred_element_type=F32).astype(BF16)
            part[slot, 1, :, cols] = jnp.dot(
                tok_all[o], wu[:, cols], preferred_element_type=F32).astype(BF16)

        sums.pair_copy(o, slot).start()

        @pl.when(i >= n_row - CLOSE)
        def _():
            finish(i - (n_row - CLOSE))

        return carry

    lax.fori_loop(0, n_row, step, 0)
    sums.sum_pair(shard(n_row - 1), (n_row - 1) % 2)

    def second(i, carry):
        @pl.when(i > 0)
        def _():
            o = shard(i)
            at.arrived(o, *cot)
            at.start_forwards(o, *cot)

        @pl.when(i >= CLOSE)
        def _():
            finish(i)

        return carry

    lax.fori_loop(0, n_row, second, 0)

    def drain(o, carry):
        at.end_forwards(o, *tok)
        at.end_forwards(o, *cot)
        keep(o).wait()
        fac_copy(o).wait()
        sums.end(o)
        shares.end(o)
        return carry

    lax.fori_loop(0, n_row, drain, 0)


def backward_kernel(
    n_row, n_col, tile,
    cot_ref, wd_ref, fac_ref, pre_out,
    cot_all, wd, part, pair_in, pair_sum, x_in, fac, pre,
    load_sem, cot_sem, fac_sem,
    pair_send, pair_recv, x_send, x_recv, act_keep, act_send, act_recv,
):
    at = Place(n_row, n_col)
    rows = cot_ref.shape[1]
    width = wd_ref.shape[0]

    def cot_load(o):
        return pltpu.make_async_copy(cot_ref.at[o], cot_all.at[o], cot_sem.at[o])

    def fac_load(o):
        return pltpu.make_async_copy(fac_ref.at[o], fac.at[o], fac_sem.at[o])

    load = pltpu.make_async_copy(wd_ref, wd, load_sem)
    cot_load(0).start()
    load.start()

    def begin(o, carry):
        @pl.when(o > 0)
        def _():
            cot_load(o).start()

        fac_load(o).start()
        return carry

    lax.fori_loop(0, n_row, begin, 0)
    at.greet(False)

    sums = Sums(at, tile, 1, part, pair_in, pair_sum, x_in,
                pair_send, pair_recv, x_send, x_recv)
    shares = Shares(at, rows, lambda o: pre.at[o], lambda to: pre_out.at[:, to],
                    act_keep, act_send, act_recv)

    def finish(o):
        sums.arrive(o)
        fac_load(o).wait()

        @pl.loop(0, width // tile)
        def _(t):
            cols = pl.ds(pl.multiple_of(t * tile, tile), tile)
            grad = sums.total(o, 0, cols)
            pre[o, 0, :, cols] = (grad * fac[o, 0, :, cols]).astype(BF16)
            pre[o, 1, :, cols] = (grad * fac[o, 1, :, cols]).astype(BF16)

        shares.start(o)

    def step(o, carry):
        cot_load(o).wait()

        @pl.when(o == 0)
        def _():
            load.wait()

        slot = o % 2

        @pl.loop(0, width // tile)
        def _(t):
            cols = pl.ds(pl.multiple_of(t * tile, tile), tile)
            part[slot, 0, :, cols] = lax.dot_general(
                cot_all[o], wd[cols, :], (((1,), (1,)), ((), ())),
                preferred_element_type=F32).astype(BF16)

        sums.pair_copy(o, slot).start()

        @pl.when(o > 0)
        def _():
            sums.sum_pair(o - 1, (o - 1) % 2)

        @pl.when(o >= LAG)
        def _():
            finish(o - LAG)

        return carry

    lax.fori_loop(0, n_row, step, 0)
    sums.sum_pair(n_row - 1, (n_row - 1) % 2)

    def rest(o, carry):
        finish(o)
        return carry

    lax.fori_loop(n_row - LAG, n_row, rest, 0)

    def drain(o, carry):
        sums.end(o)
        shares.end(o)
        return carry

    lax.fori_loop(0, n_row, drain, 0)


ANY = pl.BlockSpec(memory_space=pl.ANY)
DMA = pltpu.SemaphoreType.DMA


def sum_scratch(n_row, n_x, n_parts, rows, width):
    half = rows // 2
    return [
        pltpu.VMEM((2, n_parts, rows, width), BF16),
        pltpu.VMEM((n_row, n_parts, half, width), BF16),
        pltpu.VMEM((n_row, n_parts, half, width), BF16),
        pltpu.VMEM((n_row, n_x - 1, n_parts, half, width), BF16),
    ]


def sum_sems(n_row, n_x):
    return [
        DMA((n_row,)), DMA((n_row,)), DMA((n_row, n_x - 1)), DMA((n_row, n_x - 1)),
        DMA((n_row,)), DMA((n_row,)), DMA((n_row,)),
    ]


def params(number):
    return pltpu.CompilerParams(
        collective_id=number, has_side_effects=True, vmem_limit_bytes=56 * 1024 * 1024)


def forward_call(n_row, n_col, tile, tokens, w_gate, w_up, cotangent):
    rows, depth = tokens.shape
    width = w_gate.shape[1]
    n_x = n_col // 2
    total = n_row * rows
    return pl.pallas_call(
        functools.partial(forward_kernel, n_row, n_col, tile),
        out_shape=(
            jax.ShapeDtypeStruct((total, depth), BF16),
            jax.ShapeDtypeStruct((n_row, rows, depth), BF16),
            jax.ShapeDtypeStruct((total, width), BF16),
            jax.ShapeDtypeStruct((n_row, 2, rows // 2, width), F32),
        ),
        in_specs=[ANY] * 4,
        out_specs=[ANY] * 4,
        scratch_shapes=[
            pltpu.VMEM((n_row, rows, depth), BF16),
            pltpu.VMEM((depth, width), BF16),
            pltpu.VMEM((depth, width), BF16),
            *sum_scratch(n_row, n_x, 2, rows, width),
            pltpu.VMEM((n_row, 2, rows // 2, width), F32),
            DMA((4,)), DMA((n_row,)), DMA((n_row,)), DMA((n_row, 4)), DMA((n_row, 4)),
            DMA((n_row,)), DMA((n_row,)),
            *sum_sems(n_row, n_x),
        ],
        compiler_params=params(0),
        cost_estimate=pl.CostEstimate(
            flops=4 * total * depth * width, bytes_accessed=4 * depth * width,
            transcendentals=0),
    )(tokens, w_gate, w_up, cotangent)


def backward_call(n_row, n_col, tile, grad_rows, w_down, factors):
    _, rows, depth = grad_rows.shape
    width = w_down.shape[0]
    n_x = n_col // 2
    total = n_row * rows
    return pl.pallas_call(
        functools.partial(backward_kernel, n_row, n_col, tile),
        out_shape=jax.ShapeDtypeStruct((2, total, width), BF16),
        in_specs=[ANY] * 3,
        out_specs=ANY,
        scratch_shapes=[
            pltpu.VMEM((n_row, rows, depth), BF16),
            pltpu.VMEM((width, depth), BF16),
            *sum_scratch(n_row, n_x, 1, rows, width),
            pltpu.VMEM((n_row, 2, rows // 2, width), F32),
            pltpu.VMEM((n_row, 2, rows // 2, width), BF16),
            DMA, DMA((n_row,)), DMA((n_row,)),
            *sum_sems(n_row, n_x),
        ],
        compiler_params=params(1),
        cost_estimate=pl.CostEstimate(
            flops=2 * total * depth * width, bytes_accessed=2 * depth * width,
            transcendentals=0),
    )(grad_rows, w_down, factors)


def local(n_row, n_col, tokens, w_gate, w_up, w_down, cotangent):
    tile = 256 if w_gate.shape[1] % 256 == 0 else 128
    gathered, grad_rows, hidden, factors = forward_call(
        n_row, n_col, tile, tokens, w_gate, w_up, cotangent)
    terms = jnp.dot(hidden, w_down, preferred_element_type=F32).astype(BF16)
    terms, grad_rows = lax.optimization_barrier((terms, grad_rows))
    mixed_out = lax.psum_scatter(terms, "row", scatter_dimension=0, tiled=True)
    pre = backward_call(n_row, n_col, tile, grad_rows, w_down, factors)
    grad_rows = grad_rows.reshape(gathered.shape)
    grad_down = over_tokens(hidden, grad_rows).astype(BF16)
    grad_gate = over_tokens(gathered, pre[0]).astype(BF16)
    grad_up = over_tokens(gathered, pre[1]).astype(BF16)
    return (mixed_out, grad_gate, grad_up, grad_down)


def solution(mesh):
    n_row, n_col = mesh.shape["row"], mesh.shape["col"]
    return jax.shard_map(
        functools.partial(local, n_row, n_col),
        mesh=mesh,
        in_specs=(
            P("row", "col"),
            P("col", "row"),
            P("col", "row"),
            P("row", "col"),
            P("row", "col"),
        ),
        out_specs=(P("row", "col"), P("col", "row"), P("col", "row"), P("row", "col")),
        check_vma=False,
    )
```

time: 476 us -> 250 us (0.53)
  waiting for transfers between devices: 346 us -> 2.13 us
  Pallas kernels: 0 us -> 190 us
  matrix products: 86.2 us -> 43.1 us
  local copies, waits for them, and re-layouts: 19.9 us -> 0.02 us
  other arithmetic: 8.86 us -> 0 us
    all_gather x5 -> x0, waiting for transfers between devices: 192 us -> none  [the longest x1 77.6 us: local(): gathered = lax.all_gather(tokens, 'row', axis=0, tiled=True)]
    pallas_call x0 -> x2, Pallas kernels: none -> 190 us  [the longest x1 136 us: forward_call(): pl.pallas_call(functools.partial(forward_kernel, n_row, n_col, tile), out...]
    reduce_scatter x3 -> x1, waiting for transfers between devices: 152 us -> 2.11 us  [local(): mixed_out = lax.psum_scatter(terms, 'row', scatter_dimension=0, tiled=True)]
    dot_general x3 -> x1, matrix products: 48.6 us -> 10.7 us  [local(): terms = jnp.dot(hidden, w_down, preferred_element_type=F32).astype(BF16)]
    unnamed x2 -> x10, local copies, waits for them, and re-layouts: 19.9 us -> 0.02 us
    convert_element_type x2 -> x0, other arithmetic: 8.86 us -> none  [the longest x1 5.24 us: backward_step(): pre_up = (hidden_grad * silu_gate).astype(jnp.bfloat16)]
    dot_general x3, matrix products: 37.6 us -> 32.4 us  [over_tokens(): lax.dot_general(left, right, (((0,), (0,)), ((), ())), preferred_element_...]
  transfers between devices with their start and end apart: 8 -> 1, of which waited for: 8 -> 1; matrix products, arithmetic and copies ran while one was open for 23% -> 13% of each run, Pallas kernels for 0% -> 22%
where the time goes in v2:
time: 250 us
  Pallas kernels  190 us (76%)
  matrix products  43.1 us (17%)
  between operations  14.1 us (6%)
    pallas_call x1, Pallas kernels, forward_call(): pl.pallas_call(functools.partial(forward_kernel, n_row, n_col, tile), out...  136 us
    pallas_call x1, Pallas kernels, backward_call(): pl.pallas_call(functools.partial(backward_kernel, n_row, n_col, tile), ou...  54.7 us
    dot_general x3, matrix products, over_tokens(): lax.dot_general(left, right, (((0,), (0,)), ((), ())), preferred_element_...  32.4 us
    dot_general x1, matrix products, local(): terms = jnp.dot(hidden, w_down, preferred_element_type=F32).astype(BF16)  10.7 us
  transfers between devices with their start and end apart: 1, of which 1 were waited for; matrix products, arithmetic and copies ran while one was open for 13% of the time, Pallas kernels for 22%

profile of v2, /device:TPU:0, one launch (start us, length us, event | category | flops | bytes accessed | tf_op | source)
XLA Modules:
  0.0 249.8 jit_solution(2339562549676564593)
XLA Ops:
  7.2 0.0 reduce-scatter.2.cloned.1.call-start
  7.2 0.0 copy-start
  7.2 135.7 %shard_map.84 = (bf16[1024,2048]{1,0:T(8,128)(2,1)}, bf16[8,128,2048]{2,1,0:T(8,128)(2,1)}, bf16[1024,1792]{1,0:T(8,128)(2,1)}, f32[8,2,64,1792]{3,2,1,0:T(8,128)}) custom-call(bf16[128,2048]{1,0:T(8,128)(2,1)} %tok_ref.1, bf16[2048,1792]{1,0:T(8,128)(2,1)} %wg_ref.1, bf16[2048,1792]{1,0:T(8,128)(2,1)} %wu_ref.1, bf16[128,2048]{1,0:T(8,128)(2,1)} %cot_ref.1), custom_call_target="tpu_custom_call" | custom-call | flops 15032385536 | bytes 14680064 | tf_op jit(solution)/shard_map/pallas_call | solution.py:453
  142.9 0.0 copy-done
  142.9 10.7 %convolution_convert_fusion.3 = bf16[1024,2048]{1,0:T(8,128)(2,1)} fusion(bf16[1024,1792]{1,0:T(8,128)(2,1)} %get-tuple-element.10, bf16[1792,2048]{1,0:T(8,128)(2,1)S(1)} %copy-done), kind=kOutput, calls=%fused_computation.3 | convolution fusion | flops 7518289920 | bytes 15204352 | tf_op jit(solution)/shard_map/dot_general | solution.py:510
  153.7 0.0 reduce-scatter.2.cloned.1.call-update
  153.7 0.0 copy-start.4
  153.7 54.7 %shard_map.85 = bf16[2,1024,1792]{2,1,0:T(8,128)(2,1)} custom-call(bf16[8,128,2048]{2,1,0:T(8,128)(2,1)} %get-tuple-element.14.cot_ref, bf16[1792,2048]{1,0:T(8,128)(2,1)} %wd_ref.1, f32[8,2,64,1792]{3,2,1,0:T(8,128)} %get-tuple-element.15.fac_ref), custom_call_target="tpu_custom_call" | custom-call | flops 7516192768 | bytes 7340032 | tf_op jit(solution)/shard_map/pallas_call | solution.py:485
  208.4 0.0 copy-done.4
  208.4 0.0 copy-start.2
  208.4 12.1 %convolution_convert_fusion.1 = bf16[2048,1792]{1,0:T(8,128)(2,1)} fusion(bf16[1024,2048]{1,0:T(8,128)(2,1)S(1)} %copy-done.4, bf16[2,1024,1792]{2,1,0:T(8,128)(2,1)} %shard_map.85), kind=kOutput, calls=%fused_computation.1 | convolution fusion | flops 7519862784 | bytes 15204352 | tf_op jit(solution)/shard_map/dot_general | solution.py:19
  220.5 0.0 copy-done.2
  220.5 0.0 copy-start.1
  220.6 0.0 copy-start.3
  220.6 10.2 %convolution_convert_fusion.2 = bf16[2048,1792]{1,0:T(8,128)(2,1)} fusion(bf16[1024,2048]{1,0:T(8,128)(2,1)S(1)} %copy-done.4, bf16[2,1024,1792]{2,1,0:T(8,128)(2,1)S(1)} %copy-done.2), kind=kOutput, calls=%fused_computation.2 | convolution fusion | flops 7519862784 | bytes 15204352 | tf_op jit(solution)/shard_map/dot_general | solution.py:19
  230.8 0.0 copy-done.1
  230.8 0.0 copy-done.3
  230.8 10.0 %convolution_convert_fusion = bf16[1792,2048]{1,0:T(8,128)(2,1)} fusion(bf16[1024,1792]{1,0:T(8,128)(2,1)S(1)} %copy-done.3, bf16[1024,2048]{1,0:T(8,128)(2,1)S(1)} %bitcast.13), kind=kOutput, calls=%fused_computation | convolution fusion | flops 7519862784 | bytes 15204352 | tf_op jit(solution)/shard_map/dot_general | solution.py:19
  240.8 2.1 reduce-scatter.2.cloned.1.call-done
Async XLA Ops:
  7.2 235.8 %reduce-scatter.2.cloned.1.call-start = ((), (), s32[]{:S(2)}) async-start(), calls=%async_computation.1 | async-start | bytes 4718592 | tf_op jit(solution)/shard_map/reduce_scatter | solution.py:512
  7.2 135.7 %copy-start = (bf16[1792,2048]{1,0:T(8,128)(2,1)S(1)}, bf16[1792,2048]{1,0:T(8,128)(2,1)}, u32[]{:S(2)}) copy-start(bf16[1792,2048]{1,0:T(8,128)(2,1)} %wd_ref.1) | copy-start | bytes 22020100
  153.7 54.7 %copy-start.4 = (bf16[1024,2048]{1,0:T(8,128)(2,1)S(1)}, bf16[1024,2048]{1,0:T(8,128)(2,1)}, u32[]{:S(2)}) copy-start(bf16[1024,2048]{1,0:T(8,128)(2,1)} %get-tuple-element.13) | copy-start | bytes 12582916
  208.4 12.2 %copy-start.2 = (bf16[2,1024,1792]{2,1,0:T(8,128)(2,1)S(1)}, bf16[2,1024,1792]{2,1,0:T(8,128)(2,1)}, u32[]{:S(2)}) copy-start(bf16[2,1024,1792]{2,1,0:T(8,128)(2,1)} %shard_map.85) | copy-start | bytes 22020100
  220.5 10.2 %copy-start.1 = (bf16[8,128,2048]{2,1,0:T(8,128)(2,1)S(1)}, bf16[8,128,2048]{2,1,0:T(8,128)(2,1)}, u32[]{:S(2)}) copy-start(bf16[8,128,2048]{2,1,0:T(8,128)(2,1)} %get-tuple-element.14.cot_ref) | copy-start | bytes 12582916
  220.6 10.2 %copy-start.3 = (bf16[1024,1792]{1,0:T(8,128)(2,1)S(1)}, bf16[1024,1792]{1,0:T(8,128)(2,1)}, u32[]{:S(2)}) copy-start(bf16[1024,1792]{1,0:T(8,128)(2,1)} %get-tuple-element.10) | copy-start | bytes 11010052
Sparse Core Ops, SparseCore 0:
  153.8 89.0 reduce-scatter.1

commit v3 on v2

--- a/solution.py
+++ b/solution.py
@@ -49,17 +49,20 @@
     def peer(self, k):
         return ((self.x + k) % self.n_x) * 2 + self.core
 
-    def greet(self, with_rows):
+    def shard(self, i):
+        return (nearest(self.z, i // self.n_y, Z) * self.n_y
+                + nearest(self.y, i % self.n_y, self.n_y))
+
+    def greet(self):
         barrier = pltpu.get_barrier_semaphore()
         peers = jnp.int32(self.n_x)
-        if with_rows:
-            for there, who in self.sides:
-                peers = peers + there.astype(jnp.int32)
-
-                @pl.when(there)
-                def _():
-                    pl.semaphore_signal(
-                        barrier, inc=1, device_id=(who, self.col), device_id_type=MESH)
+        for there, who in self.sides:
+            peers = peers + there.astype(jnp.int32)
+
+            @pl.when(there)
+            def _():
+                pl.semaphore_signal(
+                    barrier, inc=1, device_id=(who, self.col), device_id_type=MESH)
         pl.semaphore_signal(
             barrier, inc=1, device_id=(self.row, self.twin), device_id_type=MESH)
         for k in range(1, self.n_x):
@@ -67,16 +70,27 @@
                 barrier, inc=1, device_id=(self.row, self.peer(k)), device_id_type=MESH)
         pl.semaphore_wait(barrier, peers)
 
-    def forwards(self, o, buf, send, recv):
+    def branches(self, o):
         zo, yo = o // self.n_y, o % self.n_y
-        whens = (
+        return (
             (yo == self.y) & (self.z >= zo) & (self.z < Z - 1),
             (yo == self.y) & (self.z <= zo) & (self.z > 0),
             (self.y >= yo) & (self.y < self.n_y - 1),
             (self.y <= yo) & (self.y > 0),
         )
+
+    def stem(self, o):
+        zo, yo = o // self.n_y, o % self.n_y
+        along_y = jnp.where(yo < self.y, self.row - 1, self.row + 1)
+        along_z = jnp.where(zo < self.z, self.row - self.n_y, self.row + self.n_y)
+        side_y = jnp.where(yo < self.y, 2, 3)
+        side_z = jnp.where(zo < self.z, 0, 1)
+        return (jnp.where(yo == self.y, along_z, along_y),
+                jnp.where(yo == self.y, side_z, side_y))
+
+    def forwards(self, o, buf, send, recv):
         out = []
-        for d, (when, (_, who)) in enumerate(zip(whens, self.sides)):
+        for d, (when, (_, who)) in enumerate(zip(self.branches(o), self.sides)):
             out.append((when, pltpu.make_async_remote_copy(
                 src_ref=buf.at[o], dst_ref=buf.at[o],
                 send_sem=send.at[o, d], recv_sem=recv.at[o],
@@ -212,7 +226,7 @@
     ]
     for load in loads:
         load.start()
-    at.greet(True)
+    at.greet()
 
     sums = Sums(at, tile, 2, part, pair_in, pair_sum, x_in,
                 pair_send, pair_recv, x_send, x_recv)
@@ -221,8 +235,7 @@
     tok = (tok_all, tok_send, tok_recv)
     cot = (cot_out, cot_send, cot_recv)
 
-    def shard(i):
-        return nearest(at.z, i // at.n_y, Z) * at.n_y + nearest(at.y, i % at.n_y, at.n_y)
+    shard = at.shard
 
     def keep(o):
         to = pl.ds(pl.multiple_of(o * rows, rows), rows)
@@ -269,7 +282,14 @@
         @pl.when(i == n_row // 2)
         def _():
             loads[3].wait()
-            at.start_forwards(at.row, *cot)
+
+        @pl.when(i > n_row // 2)
+        def _():
+            at.arrived(shard(i - n_row // 2), *cot)
+
+        @pl.when(i >= n_row // 2)
+        def _():
+            at.start_forwards(shard(i - n_row // 2), *cot)
 
         @pl.when(i == 0)
         def _():
@@ -298,7 +318,7 @@
     sums.sum_pair(shard(n_row - 1), (n_row - 1) % 2)
 
     def second(i, carry):
-        @pl.when(i > 0)
+        @pl.when(i >= n_row // 2)
         def _():
             o = shard(i)
             at.arrived(o, *cot)
@@ -326,17 +346,22 @@
 
 def backward_kernel(
     n_row, n_col, tile,
-    cot_ref, wd_ref, fac_ref, pre_out,
-    cot_all, wd, part, pair_in, pair_sum, x_in, fac, pre,
-    load_sem, cot_sem, fac_sem,
+    cot_ref, hid_ref, wd_ref, fac_ref, pre_out, mix_out,
+    cot_all, hid, wd, part, pair_in, pair_sum, x_in, fac, pre, mix, mix_in,
+    load_sem, mix_sem, cot_sem, hid_sem, fac_sem, mix_send, mix_recv,
     pair_send, pair_recv, x_send, x_recv, act_keep, act_send, act_recv,
 ):
     at = Place(n_row, n_col)
-    rows = cot_ref.shape[1]
+    rows, depth = cot_ref.shape[1:]
     width = wd_ref.shape[0]
+    wide = 256 if depth % 256 == 0 else 128
 
     def cot_load(o):
         return pltpu.make_async_copy(cot_ref.at[o], cot_all.at[o], cot_sem.at[o])
+
+    def hid_load(o):
+        return pltpu.make_async_copy(
+            hid_ref.at[pl.ds(pl.multiple_of(o * rows, rows), rows)], hid.at[o], hid_sem.at[o])
 
     def fac_load(o):
         return pltpu.make_async_copy(fac_ref.at[o], fac.at[o], fac_sem.at[o])
@@ -345,21 +370,78 @@
     cot_load(0).start()
     load.start()
 
-    def begin(o, carry):
-        @pl.when(o > 0)
-        def _():
-            cot_load(o).start()
-
-        fac_load(o).start()
+    def begin(i, carry):
+        @pl.when(i > 0)
+        def _():
+            cot_load(i).start()
+
+        hid_load(at.shard(n_row - 1 - i)).start()
+        fac_load(i).start()
         return carry
 
     lax.fori_loop(0, n_row, begin, 0)
-    at.greet(False)
+    at.greet()
 
     sums = Sums(at, tile, 1, part, pair_in, pair_sum, x_in,
                 pair_send, pair_recv, x_send, x_recv)
     shares = Shares(at, rows, lambda o: pre.at[o], lambda to: pre_out.at[:, to],
                     act_keep, act_send, act_recv)
+
+    def mix_copy(o):
+        who, side = at.stem(o)
+        return pltpu.make_async_remote_copy(
+            src_ref=mix.at[o], dst_ref=mix_in.at[o, side],
+            send_sem=mix_send.at[o], recv_sem=mix_recv.at[o, side],
+            device_id=(who, at.col), device_id_type=MESH,
+        )
+
+    def mix_arrived(o, d):
+        pltpu.make_async_remote_copy(
+            src_ref=mix.at[o], dst_ref=mix_in.at[o, d],
+            send_sem=mix_send.at[o], recv_sem=mix_recv.at[o, d],
+            device_id=(at.row, at.twin), device_id_type=MESH,
+        ).wait_recv()
+
+    def is_leaf(o):
+        b = at.branches(o)
+        return jnp.logical_not(b[0] | b[1] | b[2] | b[3])
+
+    def mix_result():
+        return pltpu.make_async_copy(mix.at[at.row], mix_out, mix_sem)
+
+    def grow(o):
+        hid_load(o).wait()
+
+        @pl.loop(0, depth // wide)
+        def _(t):
+            cols = pl.ds(pl.multiple_of(t * wide, wide), wide)
+            mix[o, :, cols] = jnp.dot(
+                hid[o], wd[:, cols], preferred_element_type=F32).astype(BF16)
+
+        @pl.when(is_leaf(o))
+        def _():
+            mix_copy(o).start()
+
+    def join(o):
+        for d, when in enumerate(at.branches(o)):
+            @pl.when(when)
+            def _():
+                mix_arrived(o, d)
+
+                @pl.loop(0, depth // wide)
+                def _(t):
+                    cols = pl.ds(pl.multiple_of(t * wide, wide), wide)
+                    mix[o, :, cols] = (
+                        mix[o, :, cols].astype(F32) + mix_in[o, d, :, cols].astype(F32)
+                    ).astype(BF16)
+
+        @pl.when(jnp.logical_not(is_leaf(o)) & (o != at.row))
+        def _():
+            mix_copy(o).start()
+
+        @pl.when(o == at.row)
+        def _():
+            mix_result().start()
 
     def finish(o):
         sums.arrive(o)
@@ -374,49 +456,49 @@
 
         shares.start(o)
 
-    def step(o, carry):
-        cot_load(o).wait()
-
-        @pl.when(o == 0)
-        def _():
-            load.wait()
-
-        slot = o % 2
-
-        @pl.loop(0, width // tile)
-        def _(t):
-            cols = pl.ds(pl.multiple_of(t * tile, tile), tile)
-            part[slot, 0, :, cols] = lax.dot_general(
-                cot_all[o], wd[cols, :], (((1,), (1,)), ((), ())),
-                preferred_element_type=F32).astype(BF16)
-
-        sums.pair_copy(o, slot).start()
-
-        @pl.when(o > 0)
-        def _():
-            sums.sum_pair(o - 1, (o - 1) % 2)
-
-        @pl.when(o >= LAG)
-        def _():
-            finish(o - LAG)
+    def step(i, carry):
+        @pl.when(i < n_row)
+        def _():
+            cot_load(i).wait()
+
+            @pl.when(i == 0)
+            def _():
+                load.wait()
+
+            slot = i % 2
+
+            @pl.loop(0, width // tile)
+            def _(t):
+                cols = pl.ds(pl.multiple_of(t * tile, tile), tile)
+                part[slot, 0, :, cols] = lax.dot_general(
+                    cot_all[i], wd[cols, :], (((1,), (1,)), ((), ())),
+                    preferred_element_type=F32).astype(BF16)
+
+            sums.pair_copy(i, slot).start()
+            grow(at.shard(n_row - 1 - i))
+            sums.sum_pair(i, slot)
+
+        @pl.when(i >= LAG)
+        def _():
+            join(at.shard(n_row - 1 - (i - LAG)))
+            finish(i - LAG)
 
         return carry
 
-    lax.fori_loop(0, n_row, step, 0)
-    sums.sum_pair(n_row - 1, (n_row - 1) % 2)
-
-    def rest(o, carry):
-        finish(o)
-        return carry
-
-    lax.fori_loop(n_row - LAG, n_row, rest, 0)
+    lax.fori_loop(0, n_row + LAG, step, 0)
 
     def drain(o, carry):
         sums.end(o)
         shares.end(o)
+
+        @pl.when(o != at.row)
+        def _():
+            mix_copy(o).wait_send()
+
         return carry
 
     lax.fori_loop(0, n_row, drain, 0)
+    mix_result().wait()
 
 
 ANY = pl.BlockSpec(memory_space=pl.ANY)
@@ -477,40 +559,45 @@
     )(tokens, w_gate, w_up, cotangent)
 
 
-def backward_call(n_row, n_col, tile, grad_rows, w_down, factors):
+def backward_call(n_row, n_col, tile, grad_rows, hidden, w_down, factors):
     _, rows, depth = grad_rows.shape
     width = w_down.shape[0]
     n_x = n_col // 2
     total = n_row * rows
     return pl.pallas_call(
         functools.partial(backward_kernel, n_row, n_col, tile),
-        out_shape=jax.ShapeDtypeStruct((2, total, width), BF16),
-        in_specs=[ANY] * 3,
-        out_specs=ANY,
+        out_shape=(
+            jax.ShapeDtypeStruct((2, total, width), BF16),
+            jax.ShapeDtypeStruct((rows, depth), BF16),
+        ),
+        in_specs=[ANY] * 4,
+        out_specs=[ANY] * 2,
         scratch_shapes=[
             pltpu.VMEM((n_row, rows, depth), BF16),
+            pltpu.VMEM((n_row, rows, width), BF16),
             pltpu.VMEM((width, depth), BF16),
             *sum_scratch(n_row, n_x, 1, rows, width),
             pltpu.VMEM((n_row, 2, rows // 2, width), F32),
             pltpu.VMEM((n_row, 2, rows // 2, width), BF16),
-            DMA, DMA((n_row,)), DMA((n_row,)),
+            pltpu.VMEM((n_row, rows, depth), BF16),
+            pltpu.VMEM((n_row, 4, rows, depth), BF16),
+            DMA, DMA, DMA((n_row,)), DMA((n_row,)), DMA((n_row,)),
+            DMA((n_row,)), DMA((n_row, 4)),
             *sum_sems(n_row, n_x),
         ],
         compiler_params=params(1),
         cost_estimate=pl.CostEstimate(
-            flops=2 * total * depth * width, bytes_accessed=2 * depth * width,
+            flops=4 * total * depth * width, bytes_accessed=2 * depth * width,
             transcendentals=0),
-    )(grad_rows, w_down, factors)
+    )(grad_rows, hidden, w_down, factors)
 
 
 def local(n_row, n_col, tokens, w_gate, w_up, w_down, cotangent):
     tile = 256 if w_gate.shape[1] % 256 == 0 else 128
     gathered, grad_rows, hidden, factors = forward_call(
         n_row, n_col, tile, tokens, w_gate, w_up, cotangent)
-    terms = jnp.dot(hidden, w_down, preferred_element_type=F32).astype(BF16)
-    terms, grad_rows = lax.optimization_barrier((terms, grad_rows))
-    mixed_out = lax.psum_scatter(terms, "row", scatter_dimension=0, tiled=True)
-    pre = backward_call(n_row, n_col, tile, grad_rows, w_down, factors)
+    pre, mixed_out = backward_call(
+        n_row, n_col, tile, grad_rows, hidden, w_down, factors)
     grad_rows = grad_rows.reshape(gathered.shape)
     grad_down = over_tokens(hidden, grad_rows).astype(BF16)
     grad_gate = over_tokens(gathered, pre[0]).astype(BF16)

time: 250 us -> 257 us (1.028); the launches traced: 250 us -> 252 us
  Pallas kernels: 190 us -> 220 us
  between operations: 14.1 us -> 0.7 us
  matrix products: 43.1 us -> 30.3 us
    pallas_call x1, Pallas kernels: 54.7 us -> 77.4 us  [backward_call(): pl.pallas_call(functools.partial(backward_kernel, n_row, n_col, tile), ou...]
    dot_general x1 -> x0, matrix products: 10.7 us -> none  [local(): terms = jnp.dot(hidden, w_down, preferred_element_type=F32).astype(BF16)]
    pallas_call x1, Pallas kernels: 136 us -> 142 us  [forward_call(): pl.pallas_call(functools.partial(forward_kernel, n_row, n_col, tile), out...]
  transfers between devices with their start and end apart: 1 -> 0, of which waited for: 1 -> 0; matrix products, arithmetic and copies ran while one was open for 13% -> 0% of each run, Pallas kernels for 22% -> 0%
where the time goes in v3:
time: 257 us; the launch traced here: 252 us
  Pallas kernels  220 us (86%)
  matrix products  30.3 us (12%)
    pallas_call x1, Pallas kernels, forward_call(): pl.pallas_call(functools.partial(forward_kernel, n_row, n_col, tile), out...  142 us
    pallas_call x1, Pallas kernels, backward_call(): pl.pallas_call(functools.partial(backward_kernel, n_row, n_col, tile), ou...  77.4 us
    dot_general x3, matrix products, over_tokens(): lax.dot_general(left, right, (((0,), (0,)), ((), ())), preferred_element_...  30.3 us

profile of v3, /device:TPU:0, one launch (start us, length us, event | category | flops | bytes accessed | tf_op | source)
XLA Modules:
  0.0 251.6 jit_solution(14840835666242398265)
XLA Ops:
  0.6 142.4 %shard_map.84 = (bf16[1024,2048]{1,0:T(8,128)(2,1)}, bf16[8,128,2048]{2,1,0:T(8,128)(2,1)}, bf16[1024,1792]{1,0:T(8,128)(2,1)}, f32[8,2,64,1792]{3,2,1,0:T(8,128)}) custom-call(bf16[128,2048]{1,0:T(8,128)(2,1)} %tok_ref.1, bf16[2048,1792]{1,0:T(8,128)(2,1)} %wg_ref.1, bf16[2048,1792]{1,0:T(8,128)(2,1)} %wu_ref.1, bf16[128,2048]{1,0:T(8,128)(2,1)} %cot_ref.1), custom_call_target="tpu_custom_call" | custom-call | flops 15032385536 | bytes 14680064 | tf_op jit(solution)/shard_map/pallas_call | solution.py:535
  143.0 0.0 copy-start.1
  143.0 0.0 copy-start.4
  143.0 77.4 %shard_map.85 = (bf16[2,1024,1792]{2,1,0:T(8,128)(2,1)}, bf16[128,2048]{1,0:T(8,128)(2,1)}) custom-call(bf16[8,128,2048]{2,1,0:T(8,128)(2,1)} %get-tuple-element.10.cot_ref, bf16[1024,1792]{1,0:T(8,128)(2,1)} %get-tuple-element.11.hid_ref, bf16[1792,2048]{1,0:T(8,128)(2,1)} %wd_ref.1, f32[8,2,64,1792]{3,2,1,0:T(8,128)} %get-tuple-element.12.fac_ref), custom_call_target="tpu_custom_call" | custom-call | flops 15032385536 | bytes 7340032 | tf_op jit(solution)/shard_map/pallas_call | solution.py:567
  220.5 0.0 copy-done.1
  220.5 0.0 copy-done.4
  220.5 0.0 copy-start.2
  220.5 0.0 copy-start.3
  220.5 9.9 %convolution_convert_fusion = bf16[1792,2048]{1,0:T(8,128)(2,1)} fusion(bf16[1024,1792]{1,0:T(8,128)(2,1)S(1)} %copy-done.4, bf16[1024,2048]{1,0:T(8,128)(2,1)S(1)} %bitcast.11), kind=kOutput, calls=%fused_computation | convolution fusion | flops 7519862784 | bytes 15204352 | tf_op jit(solution)/shard_map/dot_general | solution.py:19
  230.4 0.0 copy-done.2
  230.4 0.0 copy-done.3
  230.4 10.2 %convolution_convert_fusion.1 = bf16[2048,1792]{1,0:T(8,128)(2,1)} fusion(bf16[1024,2048]{1,0:T(8,128)(2,1)S(1)} %copy-done.3, bf16[2,1024,1792]{2,1,0:T(8,128)(2,1)S(1)} %copy-done.2), kind=kOutput, calls=%fused_computation.1 | convolution fusion | flops 7519862784 | bytes 15204352 | tf_op jit(solution)/shard_map/dot_general | solution.py:19
  240.6 0.0 copy-start
  240.6 10.2 %convolution_convert_fusion.2 = bf16[2048,1792]{1,0:T(8,128)(2,1)} fusion(bf16[1024,2048]{1,0:T(8,128)(2,1)S(1)} %copy-done.3, bf16[2,1024,1792]{2,1,0:T(8,128)(2,1)S(1)} %copy-done.2), kind=kOutput, calls=%fused_computation.2 | convolution fusion | flops 7519862784 | bytes 15204352 | tf_op jit(solution)/shard_map/dot_general | solution.py:19
  250.8 0.0 copy-done
  250.8 0.8 copy.10
Async XLA Ops:
  143.0 77.5 %copy-start.1 = (bf16[8,128,2048]{2,1,0:T(8,128)(2,1)S(1)}, bf16[8,128,2048]{2,1,0:T(8,128)(2,1)}, u32[]{:S(2)}) copy-start(bf16[8,128,2048]{2,1,0:T(8,128)(2,1)} %get-tuple-element.10.cot_ref) | copy-start | bytes 12582916
  143.0 77.5 %copy-start.4 = (bf16[1024,1792]{1,0:T(8,128)(2,1)S(1)}, bf16[1024,1792]{1,0:T(8,128)(2,1)}, u32[]{:S(2)}) copy-start(bf16[1024,1792]{1,0:T(8,128)(2,1)} %get-tuple-element.11.hid_ref) | copy-start | bytes 11010052
  220.5 9.9 %copy-start.2 = (bf16[2,1024,1792]{2,1,0:T(8,128)(2,1)S(1)}, bf16[2,1024,1792]{2,1,0:T(8,128)(2,1)}, u32[]{:S(2)}) copy-start(bf16[2,1024,1792]{2,1,0:T(8,128)(2,1)} %get-tuple-element.15) | copy-start | bytes 22020100
  220.5 9.9 %copy-start.3 = (bf16[1024,2048]{1,0:T(8,128)(2,1)S(1)}, bf16[1024,2048]{1,0:T(8,128)(2,1)}, u32[]{:S(2)}) copy-start(bf16[1024,2048]{1,0:T(8,128)(2,1)} %get-tuple-element.14) | copy-start | bytes 12582916
  240.6 10.2 %copy-start = (bf16[128,2048]{1,0:T(8,128)(2,1)S(1)}, bf16[128,2048]{1,0:T(8,128)(2,1)}, u32[]{:S(2)}) copy-start(bf16[128,2048]{1,0:T(8,128)(2,1)} %get-tuple-element.20) | copy-start | bytes 1572868

commit v4 on v2

--- a/solution.py
+++ b/solution.py
@@ -67,18 +67,25 @@
                 barrier, inc=1, device_id=(self.row, self.peer(k)), device_id_type=MESH)
         pl.semaphore_wait(barrier, peers)
 
-    def forwards(self, o, buf, send, recv):
+    def branches(self, o, along_z_first):
         zo, yo = o // self.n_y, o % self.n_y
-        whens = (
-            (yo == self.y) & (self.z >= zo) & (self.z < Z - 1),
-            (yo == self.y) & (self.z <= zo) & (self.z > 0),
+        z_next = (
+            (self.z >= zo) & (self.z < Z - 1),
+            (self.z <= zo) & (self.z > 0),
+        )
+        y_next = (
             (self.y >= yo) & (self.y < self.n_y - 1),
             (self.y <= yo) & (self.y > 0),
         )
+        if along_z_first:
+            return tuple((yo == self.y) & when for when in z_next) + y_next
+        return z_next + tuple((zo == self.z) & when for when in y_next)
+
+    def forwards(self, o, buf, cut, along_z_first, send, recv):
         out = []
-        for d, (when, (_, who)) in enumerate(zip(whens, self.sides)):
+        for d, (when, (_, who)) in enumerate(zip(self.branches(o, along_z_first), self.sides)):
             out.append((when, pltpu.make_async_remote_copy(
-                src_ref=buf.at[o], dst_ref=buf.at[o],
+                src_ref=buf.at[o, cut], dst_ref=buf.at[o, cut],
                 send_sem=send.at[o, d], recv_sem=recv.at[o],
                 device_id=(who, self.col), device_id_type=MESH,
             )))
@@ -96,9 +103,9 @@
             def _():
                 copy.wait_send()
 
-    def arrived(self, o, buf, send, recv):
+    def arrived(self, o, buf, cut, along_z_first, send, recv):
         pltpu.make_async_remote_copy(
-            src_ref=buf.at[o], dst_ref=buf.at[o],
+            src_ref=buf.at[o, cut], dst_ref=buf.at[o, cut],
             send_sem=send.at[o, 0], recv_sem=recv.at[o],
             device_id=(self.row, self.twin), device_id_type=MESH,
         ).wait_recv()
@@ -197,7 +204,7 @@
     tok_ref, wg_ref, wu_ref, cot_ref,
     tok_out, cot_out, hid_out, fac_out,
     tok_all, wg, wu, part, pair_in, pair_sum, x_in, fac,
-    load_sem, tok_recv, cot_recv, tok_send, cot_send, keep_sem, fac_sem,
+    load_sem, tok_recv, cot_recv, alt_recv, tok_send, cot_send, alt_send, keep_sem, fac_sem,
     pair_send, pair_recv, x_send, x_recv, act_keep, act_send, act_recv,
 ):
     at = Place(n_row, n_col)
@@ -218,8 +225,10 @@
                 pair_send, pair_recv, x_send, x_recv)
     shares = Shares(at, rows, lambda o: x_in.at[o, 0, 0], lambda to: hid_out.at[to],
                     act_keep, act_send, act_recv)
-    tok = (tok_all, tok_send, tok_recv)
-    cot = (cot_out, cot_send, cot_recv)
+    most = rows - rows // 4
+    tok = (tok_all, pl.ds(0, rows), True, tok_send, tok_recv)
+    cot = (cot_out, pl.ds(0, most), True, cot_send, cot_recv)
+    alt = (cot_out, pl.ds(most, rows - most), False, alt_send, alt_recv)
 
     def shard(i):
         return nearest(at.z, i // at.n_y, Z) * at.n_y + nearest(at.y, i % at.n_y, at.n_y)
@@ -270,6 +279,7 @@
         def _():
             loads[3].wait()
             at.start_forwards(at.row, *cot)
+            at.start_forwards(at.row, *alt)
 
         @pl.when(i == 0)
         def _():
@@ -301,6 +311,8 @@
         @pl.when(i > 0)
         def _():
             o = shard(i)
+            at.arrived(o, *alt)
+            at.start_forwards(o, *alt)
             at.arrived(o, *cot)
             at.start_forwards(o, *cot)
 
@@ -315,6 +327,7 @@
     def drain(o, carry):
         at.end_forwards(o, *tok)
         at.end_forwards(o, *cot)
+        at.end_forwards(o, *alt)
         keep(o).wait()
         fac_copy(o).wait()
         sums.end(o)
@@ -466,7 +479,8 @@
             pltpu.VMEM((depth, width), BF16),
             *sum_scratch(n_row, n_x, 2, rows, width),
             pltpu.VMEM((n_row, 2, rows // 2, width), F32),
-            DMA((4,)), DMA((n_row,)), DMA((n_row,)), DMA((n_row, 4)), DMA((n_row, 4)),
+            DMA((4,)), DMA((n_row,)), DMA((n_row,)), DMA((n_row,)),
+            DMA((n_row, 4)), DMA((n_row, 4)), DMA((n_row, 4)),
             DMA((n_row,)), DMA((n_row,)),
             *sum_sems(n_row, n_x),
         ],

time: 250 us -> 253 us (1.012)
  waiting for transfers between devices: 2.13 us -> 13 us
  Pallas kernels: 190 us -> 182 us
    reduce_scatter x1, waiting for transfers between devices: 2.11 us -> 13 us  [local(): mixed_out = lax.psum_scatter(terms, 'row', scatter_dimension=0, tiled=True)]
    pallas_call x1, Pallas kernels: 136 us -> 128 us  [forward_call(): pl.pallas_call(functools.partial(forward_kernel, n_row, n_col, tile), out...]
where the time goes in v4:
time: 253 us
  Pallas kernels  182 us (72%)
  matrix products  43.2 us (17%)
  between operations  14.1 us (6%)
  waiting for transfers between devices  13 us (5%)
    pallas_call x1, Pallas kernels, forward_call(): pl.pallas_call(functools.partial(forward_kernel, n_row, n_col, tile), out...  128 us
    pallas_call x1, Pallas kernels, backward_call(): pl.pallas_call(functools.partial(backward_kernel, n_row, n_col, tile), ou...  54.7 us
    dot_general x3, matrix products, over_tokens(): lax.dot_general(left, right, (((0,), (0,)), ((), ())), preferred_element_...  32.5 us
    reduce_scatter x1, waiting for transfers between devices, local(): mixed_out = lax.psum_scatter(terms, 'row', scatter_dimension=0, tiled=True)  13 us
    dot_general x1, matrix products, local(): terms = jnp.dot(hidden, w_down, preferred_element_type=F32).astype(BF16)  10.7 us
  transfers between devices with their start and end apart: 1, of which 1 were waited for; matrix products, arithmetic and copies ran while one was open for 13% of the time, Pallas kernels for 22%

profile of v4, /device:TPU:0, one launch (start us, length us, event | category | flops | bytes accessed | tf_op | source)
XLA Modules:
  0.0 252.7 jit_solution(9930123969355500634)
XLA Ops:
  7.2 0.0 reduce-scatter.2.cloned.1.call-start
  7.2 0.0 copy-start
  7.2 127.7 %shard_map.84 = (bf16[1024,2048]{1,0:T(8,128)(2,1)}, bf16[8,128,2048]{2,1,0:T(8,128)(2,1)}, bf16[1024,1792]{1,0:T(8,128)(2,1)}, f32[8,2,64,1792]{3,2,1,0:T(8,128)}) custom-call(bf16[128,2048]{1,0:T(8,128)(2,1)} %tok_ref.1, bf16[2048,1792]{1,0:T(8,128)(2,1)} %wg_ref.1, bf16[2048,1792]{1,0:T(8,128)(2,1)} %wu_ref.1, bf16[128,2048]{1,0:T(8,128)(2,1)} %cot_ref.1), custom_call_target="tpu_custom_call" | custom-call | flops 15032385536 | bytes 14680064 | tf_op jit(solution)/shard_map/pallas_call | solution.py:466
  134.9 0.0 copy-done
  134.9 10.7 %convolution_convert_fusion.3 = bf16[1024,2048]{1,0:T(8,128)(2,1)} fusion(bf16[1024,1792]{1,0:T(8,128)(2,1)} %get-tuple-element.10, bf16[1792,2048]{1,0:T(8,128)(2,1)S(1)} %copy-done), kind=kOutput, calls=%fused_computation.3 | convolution fusion | flops 7518289920 | bytes 15204352 | tf_op jit(solution)/shard_map/dot_general | solution.py:524
  145.7 0.0 reduce-scatter.2.cloned.1.call-update
  145.7 0.0 copy-start.4
  145.7 54.7 %shard_map.85 = bf16[2,1024,1792]{2,1,0:T(8,128)(2,1)} custom-call(bf16[8,128,2048]{2,1,0:T(8,128)(2,1)} %get-tuple-element.14.cot_ref, bf16[1792,2048]{1,0:T(8,128)(2,1)} %wd_ref.1, f32[8,2,64,1792]{3,2,1,0:T(8,128)} %get-tuple-element.15.fac_ref), custom_call_target="tpu_custom_call" | custom-call | flops 7516192768 | bytes 7340032 | tf_op jit(solution)/shard_map/pallas_call | solution.py:499
  200.4 0.0 copy-done.4
  200.4 0.0 copy-start.2
  200.4 12.2 %convolution_convert_fusion.1 = bf16[2048,1792]{1,0:T(8,128)(2,1)} fusion(bf16[1024,2048]{1,0:T(8,128)(2,1)S(1)} %copy-done.4, bf16[2,1024,1792]{2,1,0:T(8,128)(2,1)} %shard_map.85), kind=kOutput, calls=%fused_computation.1 | convolution fusion | flops 7519862784 | bytes 15204352 | tf_op jit(solution)/shard_map/dot_general | solution.py:19
  212.6 0.0 copy-done.2
  212.6 0.0 copy-start.1
  212.6 0.0 copy-start.3
  212.6 10.2 %convolution_convert_fusion.2 = bf16[2048,1792]{1,0:T(8,128)(2,1)} fusion(bf16[1024,2048]{1,0:T(8,128)(2,1)S(1)} %copy-done.4, bf16[2,1024,1792]{2,1,0:T(8,128)(2,1)S(1)} %copy-done.2), kind=kOutput, calls=%fused_computation.2 | convolution fusion | flops 7519862784 | bytes 15204352 | tf_op jit(solution)/shard_map/dot_general | solution.py:19
  222.9 0.0 copy-done.1
  222.9 0.0 copy-done.3
  222.9 10.0 %convolution_convert_fusion = bf16[1792,2048]{1,0:T(8,128)(2,1)} fusion(bf16[1024,1792]{1,0:T(8,128)(2,1)S(1)} %copy-done.3, bf16[1024,2048]{1,0:T(8,128)(2,1)S(1)} %bitcast.13), kind=kOutput, calls=%fused_computation | convolution fusion | flops 7519862784 | bytes 15204352 | tf_op jit(solution)/shard_map/dot_general | solution.py:19
  232.9 13.0 %reduce-scatter.2.cloned.1.call-done = bf16[128,2048]{1,0:T(8,128)(2,1)} async-done(((bf16[1024,2048]{1,0:T(8,128)(2,1)}), bf16[128,2048]{1,0:T(8,128)(2,1)}) %reduce-scatter.2.cloned.1.call-update) | async-done | bytes 524304 | tf_op jit(solution)/shard_map/reduce_scatter | solution.py:526
Async XLA Ops:
  7.2 238.7 %reduce-scatter.2.cloned.1.call-start = ((), (), s32[]{:S(2)}) async-start(), calls=%async_computation.1 | async-start | bytes 4718592 | tf_op jit(solution)/shard_map/reduce_scatter | solution.py:526
  7.2 127.7 %copy-start = (bf16[1792,2048]{1,0:T(8,128)(2,1)S(1)}, bf16[1792,2048]{1,0:T(8,128)(2,1)}, u32[]{:S(2)}) copy-start(bf16[1792,2048]{1,0:T(8,128)(2,1)} %wd_ref.1) | copy-start | bytes 22020100
  145.7 54.7 %copy-start.4 = (bf16[1024,2048]{1,0:T(8,128)(2,1)S(1)}, bf16[1024,2048]{1,0:T(8,128)(2,1)}, u32[]{:S(2)}) copy-start(bf16[1024,2048]{1,0:T(8,128)(2,1)} %get-tuple-element.13) | copy-start | bytes 12582916
  200.4 12.2 %copy-start.2 = (bf16[2,1024,1792]{2,1,0:T(8,128)(2,1)S(1)}, bf16[2,1024,1792]{2,1,0:T(8,128)(2,1)}, u32[]{:S(2)}) copy-start(bf16[2,1024,1792]{2,1,0:T(8,128)(2,1)} %shard_map.85) | copy-start | bytes 22020100
  212.6 10.2 %copy-start.1 = (bf16[8,128,2048]{2,1,0:T(8,128)(2,1)S(1)}, bf16[8,128,2048]{2,1,0:T(8,128)(2,1)}, u32[]{:S(2)}) copy-start(bf16[8,128,2048]{2,1,0:T(8,128)(2,1)} %get-tuple-element.14.cot_ref) | copy-start | bytes 12582916
  212.6 10.2 %copy-start.3 = (bf16[1024,1792]{1,0:T(8,128)(2,1)S(1)}, bf16[1024,1792]{1,0:T(8,128)(2,1)}, u32[]{:S(2)}) copy-start(bf16[1024,1792]{1,0:T(8,128)(2,1)} %get-tuple-element.10) | copy-start | bytes 11010052
Sparse Core Ops, SparseCore 0:
  145.8 100.0 reduce-scatter.1
